TPU v7x, 32 devices: a whole 2x2x4 slice. The times are simulated.
32 devices in a mesh: row: 4 (over y, core), col: 2 (over x), fsdp: 4 (over z).
Axes of the slice: x: 2, y: 2, z: 4, core: 2. Of those that a mesh axis runs over, the one named last changes fastest.
Arguments:
- master: float32 [4, 2, 96, 4096], P('row', 'col', 'fsdp'), may hold values from -6 to 6
- moment_one: float32 [4, 2, 96, 4096], P('row', 'col', 'fsdp'), may hold values from -3 to 3
- moment_two: float32 [4, 2, 96, 4096], P('row', 'col', 'fsdp'), may hold values from 0.01 to 1
- grads: bfloat16 [4, 2, 96, 4096], P('row', 'col', 'fsdp'), may hold values from -6 to 6
- counts: int32 [4, 2, 8], P('row', 'col'), may hold values from 1 to 4095
- step: int32 [1], replicated, may hold values from 1 to 15
Outputs:
- new_master: float32 [4, 2, 96, 4096], P('row', 'col', 'fsdp')
- new_moment_one: float32 [4, 2, 96, 4096], P('row', 'col', 'fsdp')
- new_moment_two: float32 [4, 2, 96, 4096], P('row', 'col', 'fsdp')
- replica_weights: bfloat16 [4, 2, 4, 96, 4096], P('row', 'col', 'fsdp')
All inputs are finite; a program needn't handle non-finite values.
Results may differ from a plain program's by a relative error of at most 0.001.
Values may be sent and summed in bfloat16 or wider, within the bound.
No kernel may reach another device: no remote copies, remote signals or barrier semaphores. Data moves between devices by JAX's collectives and lax.ppermute only.
A program may use at most 64 MiB of HBM per device.

v0:
```python
import jax
import jax.numpy as jnp
from jax import lax
from jax.sharding import PartitionSpec as P


def passed_along(block, axis, distance):
    devices = range(lax.axis_size(axis))
    route = [((i - distance) % len(devices), i) for i in devices]
    return lax.ppermute(block, axis, route)


def row_round(states, weight):
    sent = (weight * states[0], weight * states[1], weight * states[2], weight)
    below = passed_along((sent[0], sent[1], sent[2], sent[3]), "row", 1)
    above = passed_along((sent[0], sent[1], sent[2], sent[3]), "row", -1)
    total = below[3] + weight + above[3]
    merged = tuple(((below[i] + sent[i] + above[i]) / total for i in range(3)))
    return (merged, total / 3.0)


def col_round(states, weight):
    sent = (weight * states[0], weight * states[1], weight * states[2], weight)
    below = passed_along((sent[0], sent[1], sent[2], sent[3]), "col", 1)
    above = passed_along((sent[0], sent[1], sent[2], sent[3]), "col", -1)
    total = below[3] + weight + above[3]
    merged = tuple(((below[i] + sent[i] + above[i]) / total for i in range(3)))
    return merged


def finish(states, weight):
    after_row, mass = row_round(states, weight)
    after_col = col_round(after_row, mass)
    rounded = after_col[0].astype(jnp.bfloat16)
    whole = lax.all_gather(rounded, "fsdp", axis=2, tiled=True)
    return (after_col, whole[:, :, None])


def per_device(master, moment_one, moment_two, grads, counts, step):
    steps_f = step[0].astype(jnp.float32)
    grad_f = grads.astype(jnp.float32)
    first = 0.9 * moment_one + 0.1 * grad_f
    second = 0.95 * moment_two + 0.05 * grad_f * grad_f
    first_hat = first / (1.0 - jnp.power(jnp.float32(0.9), steps_f))
    second_hat = second / (1.0 - jnp.power(jnp.float32(0.95), steps_f))
    updated = master - 0.1 * (first_hat / (jnp.sqrt(second_hat) + 1e-08) + 0.1 * master)
    lengths = 256.0 * jnp.power(2.0, jnp.arange(counts.shape[2]).astype(jnp.float32))
    weight = jnp.sum(counts.astype(jnp.float32) * lengths, axis=-1)[:, :, None, None]
    states, copies = finish((updated, first, second), weight)
    return (states[0], states[1], states[2], copies)


def solution(mesh):
    return jax.shard_map(
        per_device,
        mesh=mesh,
        in_specs=(
            P("row", "col", "fsdp", None),
            P("row", "col", "fsdp", None),
            P("row", "col", "fsdp", None),
            P("row", "col", "fsdp", None),
            P("row", "col", None),
            P(),
        ),
        out_specs=(
            P("row", "col", "fsdp", None),
            P("row", "col", "fsdp", None),
            P("row", "col", "fsdp", None),
            P("row", "col", "fsdp", None, None),
        ),
        check_vma=False,
    )
```

profile of v0, /device:TPU:0, one launch (start us, length us, event | category | flops | bytes accessed | tf_op | source)
XLA Modules:
  0.0 70.3 jit_solution(15457423363043766060)
XLA Ops:
  1.4 0.0 copy-start
  1.4 0.6 copy-done
  2.0 0.6 multiply_reduce_fusion
  2.6 2.3 %fusion.6 = (f32[1,1,24,4096]{3,2,1,0:T(8,128)S(1)}, f32[1,1,24,4096]{3,2,1,0:T(8,128)S(1)}, f32[1,1,24,4096]{3,2,1,0:T(8,128)S(1)}) fusion(bf16[1,1,24,4096]{3,2,1,0:T(8,128)(2,1)} %param.9, f32[1,1,24,4096]{3,2,1,0:T(8,128)} %param.8, f32[]{:T(128)} %multiply_reduce_fusion, f32[1,1,24,4096]{3,2,1,0:T(8,128)} %param.6, f32[]{:T(128)} %bitcast.3, ...), kind=kLoop, calls=%fused_computation.15 | loop fusion | flops 1867776 | bytes 2555916 | tf_op jit(solution)/shard_map/mul | solution.py:14
  5.0 2.5 %collective-permute-start.10 = (f32[1,1,24,4096]{3,2,1,0:T(8,128)S(1)}, f32[1,1,24,4096]{3,2,1,0:T(8,128)S(1)}, u32[]{:S(2)}, u32[]{:S(2)}) collective-permute-start(f32[1,1,24,4096]{3,2,1,0:T(8,128)S(1)} %get-tuple-element.6), channel_id=1, source_target_pairs={{8,0},{16,8},{24,16},{0,24},{9,1},{17,9},{25,17},{1,25},{10,2},{18... | collective-permute-start | bytes 1179656 | tf_op jit(solution)/shard_map/ppermute | solution.py:10
  7.4 0.0 collective-permute-start.9
  7.4 1.7 %collective-permute-start.1 = (f32[1,1,1,1]{3,2,1,0:T(1,128)}, f32[1,1,1,1]{3,2,1,0:T(1,128)}, u32[]{:S(2)}, u32[]{:S(2)}) collective-permute-start(f32[1,1,1,1]{3,2,1,0:T(1,128)} %bitcast), channel_id=1, source_target_pairs={{8,0},{16,8},{24,16},{0,24},{9,1},{17,9},{25,17},{1,25},{10,2},{18... | collective-permute-start | bytes 20 | tf_op jit(solution)/shard_map/ppermute | solution.py:10
  9.2 0.0 collective-permute-start
  9.2 1.7 %collective-permute-start.3 = (f32[1,1,24,4096]{3,2,1,0:T(8,128)S(1)}, f32[1,1,24,4096]{3,2,1,0:T(8,128)S(1)}, u32[]{:S(2)}, u32[]{:S(2)}) collective-permute-start(f32[1,1,24,4096]{3,2,1,0:T(8,128)S(1)} %get-tuple-element.7), channel_id=1, source_target_pairs={{8,0},{16,8},{24,16},{0,24},{9,1},{17,9},{25,17},{1,25},{10,2},{18... | collective-permute-start | bytes 1179656 | tf_op jit(solution)/shard_map/ppermute | solution.py:10
  10.9 8.0 %collective-permute-done = f32[1,1,1,1]{3,2,1,0:T(1,128)} collective-permute-done((f32[1,1,1,1]{3,2,1,0:T(1,128)}, f32[1,1,1,1]{3,2,1,0:T(1,128)}, u32[]{:S(2)}, u32[]{:S(2)}) %collective-permute-start) | collective-permute-done | bytes 36 | tf_op jit(solution)/shard_map/ppermute | solution.py:10
  18.9 0.0 collective-permute-start.2
  20.1 0.0 collective-permute-done.1
  20.8 2.9 %collective-permute-start.5 = (f32[1,1,1,1]{3,2,1,0:T(1,128)}, f32[1,1,1,1]{3,2,1,0:T(1,128)}, u32[]{:S(2)}, u32[]{:S(2)}) collective-permute-start(f32[1,1,1,1]{3,2,1,0:T(1,128)} %div.60), channel_id=1, source_target_pairs={{4,0},{0,4},{5,1},{1,5},{6,2},{2,6},{7,3},{3,7},{12,8},{8,12},{13,... | collective-permute-start | bytes 20 | tf_op jit(solution)/shard_map/ppermute | solution.py:10
  23.6 0.9 %collective-permute-done.5 = f32[1,1,1,1]{3,2,1,0:T(1,128)} collective-permute-done((f32[1,1,1,1]{3,2,1,0:T(1,128)}, f32[1,1,1,1]{3,2,1,0:T(1,128)}, u32[]{:S(2)}, u32[]{:S(2)}) %collective-permute-start.5) | collective-permute-done | bytes 36 | tf_op jit(solution)/shard_map/ppermute | solution.py:10
  24.5 0.8 %collective-permute-start.7 = (f32[1,1,24,4096]{3,2,1,0:T(8,128)S(1)}, f32[1,1,24,4096]{3,2,1,0:T(8,128)S(1)}, u32[]{:S(2)}, u32[]{:S(2)}) collective-permute-start(f32[1,1,24,4096]{3,2,1,0:T(8,128)S(1)} %get-tuple-element.8), channel_id=1, source_target_pairs={{8,0},{16,8},{24,16},{0,24},{9,1},{17,9},{25,17},{1,25},{10,2},{18... | collective-permute-start | bytes 1179656 | tf_op jit(solution)/shard_map/ppermute | solution.py:10
  26.5 0.0 collective-permute-done.10
  26.5 0.1 collective-permute-start.6
  26.6 0.0 collective-permute-done.9
  26.6 0.1 divide_multiply_fusion
  26.7 1.6 %collective-permute-start.11 = (f32[1,1,24,4096]{3,2,1,0:T(8,128)S(1)}, f32[1,1,24,4096]{3,2,1,0:T(8,128)S(1)}, u32[]{:S(2)}, u32[]{:S(2)}) collective-permute-start(f32[1,1,24,4096]{3,2,1,0:T(8,128)S(1)} %divide_multiply_fusion), channel_id=1, source_target_pairs={{4,0},{0,4},{5,1},{1,5},{6,2},{2,6},{7,3},{3,7},{12,8},{8,12},{13,... | collective-permute-start | bytes 1179656 | tf_op jit(solution)/shard_map/ppermute | solution.py:10
  28.3 0.0 collective-permute-done.3
  28.3 0.0 collective-permute-done.2
  28.3 0.1 divide_multiply_fusion.2
  28.4 0.6 collective-permute-start.4
  29.0 4.4 %collective-permute-done.7 = f32[1,1,24,4096]{3,2,1,0:T(8,128)S(1)} collective-permute-done((f32[1,1,24,4096]{3,2,1,0:T(8,128)S(1)}, f32[1,1,24,4096]{3,2,1,0:T(8,128)S(1)}, u32[]{:S(2)}, u32[]{:S(2)}) %collective-permute-start.7) | collective-permute-done | bytes 393248 | tf_op jit(solution)/shard_map/ppermute | solution.py:10
  33.3 2.6 %collective-permute-done.6 = f32[1,1,24,4096]{3,2,1,0:T(8,128)S(1)} collective-permute-done((f32[1,1,24,4096]{3,2,1,0:T(8,128)S(1)}, f32[1,1,24,4096]{3,2,1,0:T(8,128)S(1)}, u32[]{:S(2)}, u32[]{:S(2)}) %collective-permute-start.6) | collective-permute-done | bytes 393248 | tf_op jit(solution)/shard_map/ppermute | solution.py:10
  35.9 0.1 divide_multiply_fusion.1
  35.9 1.6 %collective-permute-start.8 = (f32[1,1,24,4096]{3,2,1,0:T(8,128)S(1)}, f32[1,1,24,4096]{3,2,1,0:T(8,128)S(1)}, u32[]{:S(2)}, u32[]{:S(2)}) collective-permute-start(f32[1,1,24,4096]{3,2,1,0:T(8,128)S(1)} %divide_multiply_fusion.1), channel_id=1, source_target_pairs={{4,0},{0,4},{5,1},{1,5},{6,2},{2,6},{7,3},{3,7},{12,8},{8,12},{13,... | collective-permute-start | bytes 1179656 | tf_op jit(solution)/shard_map/ppermute | solution.py:10
  37.5 9.7 %collective-permute-done.4 = f32[1,1,24,4096]{3,2,1,0:T(8,128)S(1)} collective-permute-done((f32[1,1,24,4096]{3,2,1,0:T(8,128)S(1)}, f32[1,1,24,4096]{3,2,1,0:T(8,128)S(1)}, u32[]{:S(2)}, u32[]{:S(2)}) %collective-permute-start.4) | collective-permute-done | bytes 393248 | tf_op jit(solution)/shard_map/ppermute | solution.py:10
  47.2 0.8 %fusion.7 = (bf16[1,1,24,4096]{3,2,1,0:T(8,128)(2,1)S(1)}, f32[1,1,24,4096]{3,2,1,0:T(8,128)}) fusion(f32[]{:T(128)} %bitcast.5, f32[1,1,24,4096]{3,2,1,0:T(8,128)S(1)} %collective-permute-done.4, f32[1,1,24,4096]{3,2,1,0:T(8,128)S(1)} %divide_multiply_fusion.2), kind=kLoop, calls=%fused_computation.17 | loop fusion | flops 393216 | bytes 1376260 | tf_op jit(solution)/shard_map/convert_element_type | solution.py:34
  48.0 0.0 collective-permute-done.11
  48.0 0.8 %fusion.4 = f32[1,1,24,4096]{3,2,1,0:T(8,128)} fusion(f32[1,1,24,4096]{3,2,1,0:T(8,128)S(1)} %collective-permute-done.11, f32[1,1,24,4096]{3,2,1,0:T(8,128)S(1)} %divide_multiply_fusion, f32[]{:T(128)} %bitcast.5), kind=kLoop, calls=%fused_computation.9 | loop fusion | flops 294912 | bytes 1179652 | tf_op jit(solution)/shard_map/div | solution.py:27
  48.8 19.9 %all_gather.3 = bf16[1,1,96,4096]{3,2,1,0:T(8,128)(2,1)S(1)} all-gather(bf16[1,1,24,4096]{3,2,1,0:T(8,128)(2,1)S(1)} %get-tuple-element.4), channel_id=1, replica_groups=mesh['row'=4,'col'=2,'fsdp'=4] {'fsdp'}, dimensions={2}, use_global_device_ids=true | all-gather | bytes 983040 | tf_op jit(solution)/shard_map/all_gather | solution.py:35
  68.7 0.0 collective-permute-done.8
  68.7 0.8 %fusion.3 = f32[1,1,24,4096]{3,2,1,0:T(8,128)} fusion(f32[1,1,24,4096]{3,2,1,0:T(8,128)S(1)} %collective-permute-done.8, f32[1,1,24,4096]{3,2,1,0:T(8,128)S(1)} %divide_multiply_fusion.1, f32[]{:T(128)} %bitcast.5), kind=kLoop, calls=%fused_computation.8 | loop fusion | flops 294912 | bytes 1179652 | tf_op jit(solution)/shard_map/div | solution.py:27
  69.5 0.9 %copy.12 = bf16[1,1,1,96,4096]{4,3,2,1,0:T(8,128)(2,1)} copy(bf16[1,1,1,96,4096]{4,3,2,1,0:T(8,128)(2,1)S(1)} %bitcast.7) | data formatting | bytes 1572864
Async XLA Ops:
  1.4 0.7 copy-start
  5.0 21.6 %collective-permute-start.10 = (f32[1,1,24,4096]{3,2,1,0:T(8,128)S(1)}, f32[1,1,24,4096]{3,2,1,0:T(8,128)S(1)}, u32[]{:S(2)}, u32[]{:S(2)}) collective-permute-start(f32[1,1,24,4096]{3,2,1,0:T(8,128)S(1)} %get-tuple-element.6), channel_id=1, source_target_pairs={{8,0},{16,8},{24,16},{0,24},{9,1},{17,9},{25,17},{1,25},{10,2},{18... | collective-permute-start | bytes 1179656 | tf_op jit(solution)/shard_map/ppermute | solution.py:10
  7.4 19.2 %collective-permute-start.9 = (f32[1,1,24,4096]{3,2,1,0:T(8,128)S(1)}, f32[1,1,24,4096]{3,2,1,0:T(8,128)S(1)}, u32[]{:S(2)}, u32[]{:S(2)}) collective-permute-start(f32[1,1,24,4096]{3,2,1,0:T(8,128)S(1)} %get-tuple-element.6), channel_id=1, source_target_pairs={{24,0},{0,8},{8,16},{16,24},{25,1},{1,9},{9,17},{17,25},{26,2},{2,... | collective-permute-start | bytes 1179656 | tf_op jit(solution)/shard_map/ppermute | solution.py:10
  7.4 12.7 %collective-permute-start.1 = (f32[1,1,1,1]{3,2,1,0:T(1,128)}, f32[1,1,1,1]{3,2,1,0:T(1,128)}, u32[]{:S(2)}, u32[]{:S(2)}) collective-permute-start(f32[1,1,1,1]{3,2,1,0:T(1,128)} %bitcast), channel_id=1, source_target_pairs={{8,0},{16,8},{24,16},{0,24},{9,1},{17,9},{25,17},{1,25},{10,2},{18... | collective-permute-start | bytes 20 | tf_op jit(solution)/shard_map/ppermute | solution.py:10
  9.2 9.7 %collective-permute-start = (f32[1,1,1,1]{3,2,1,0:T(1,128)}, f32[1,1,1,1]{3,2,1,0:T(1,128)}, u32[]{:S(2)}, u32[]{:S(2)}) collective-permute-start(f32[1,1,1,1]{3,2,1,0:T(1,128)} %bitcast), channel_id=1, source_target_pairs={{24,0},{0,8},{8,16},{16,24},{25,1},{1,9},{9,17},{17,25},{26,2},{2,... | collective-permute-start | bytes 20 | tf_op jit(solution)/shard_map/ppermute | solution.py:10
  9.2 19.1 %collective-permute-start.3 = (f32[1,1,24,4096]{3,2,1,0:T(8,128)S(1)}, f32[1,1,24,4096]{3,2,1,0:T(8,128)S(1)}, u32[]{:S(2)}, u32[]{:S(2)}) collective-permute-start(f32[1,1,24,4096]{3,2,1,0:T(8,128)S(1)} %get-tuple-element.7), channel_id=1, source_target_pairs={{8,0},{16,8},{24,16},{0,24},{9,1},{17,9},{25,17},{1,25},{10,2},{18... | collective-permute-start | bytes 1179656 | tf_op jit(solution)/shard_map/ppermute | solution.py:10
  18.9 9.4 %collective-permute-start.2 = (f32[1,1,24,4096]{3,2,1,0:T(8,128)S(1)}, f32[1,1,24,4096]{3,2,1,0:T(8,128)S(1)}, u32[]{:S(2)}, u32[]{:S(2)}) collective-permute-start(f32[1,1,24,4096]{3,2,1,0:T(8,128)S(1)} %get-tuple-element.7), channel_id=1, source_target_pairs={{24,0},{0,8},{8,16},{16,24},{25,1},{1,9},{9,17},{17,25},{26,2},{2,... | collective-permute-start | bytes 1179656 | tf_op jit(solution)/shard_map/ppermute | solution.py:10
  20.8 3.7 %collective-permute-start.5 = (f32[1,1,1,1]{3,2,1,0:T(1,128)}, f32[1,1,1,1]{3,2,1,0:T(1,128)}, u32[]{:S(2)}, u32[]{:S(2)}) collective-permute-start(f32[1,1,1,1]{3,2,1,0:T(1,128)} %div.60), channel_id=1, source_target_pairs={{4,0},{0,4},{5,1},{1,5},{6,2},{2,6},{7,3},{3,7},{12,8},{8,12},{13,... | collective-permute-start | bytes 20 | tf_op jit(solution)/shard_map/ppermute | solution.py:10
  24.5 8.8 %collective-permute-start.7 = (f32[1,1,24,4096]{3,2,1,0:T(8,128)S(1)}, f32[1,1,24,4096]{3,2,1,0:T(8,128)S(1)}, u32[]{:S(2)}, u32[]{:S(2)}) collective-permute-start(f32[1,1,24,4096]{3,2,1,0:T(8,128)S(1)} %get-tuple-element.8), channel_id=1, source_target_pairs={{8,0},{16,8},{24,16},{0,24},{9,1},{17,9},{25,17},{1,25},{10,2},{18... | collective-permute-start | bytes 1179656 | tf_op jit(solution)/shard_map/ppermute | solution.py:10
  26.5 9.3 %collective-permute-start.6 = (f32[1,1,24,4096]{3,2,1,0:T(8,128)S(1)}, f32[1,1,24,4096]{3,2,1,0:T(8,128)S(1)}, u32[]{:S(2)}, u32[]{:S(2)}) collective-permute-start(f32[1,1,24,4096]{3,2,1,0:T(8,128)S(1)} %get-tuple-element.8), channel_id=1, source_target_pairs={{24,0},{0,8},{8,16},{16,24},{25,1},{1,9},{9,17},{17,25},{26,2},{2,... | collective-permute-start | bytes 1179656 | tf_op jit(solution)/shard_map/ppermute | solution.py:10
  26.7 21.3 %collective-permute-start.11 = (f32[1,1,24,4096]{3,2,1,0:T(8,128)S(1)}, f32[1,1,24,4096]{3,2,1,0:T(8,128)S(1)}, u32[]{:S(2)}, u32[]{:S(2)}) collective-permute-start(f32[1,1,24,4096]{3,2,1,0:T(8,128)S(1)} %divide_multiply_fusion), channel_id=1, source_target_pairs={{4,0},{0,4},{5,1},{1,5},{6,2},{2,6},{7,3},{3,7},{12,8},{8,12},{13,... | collective-permute-start | bytes 1179656 | tf_op jit(solution)/shard_map/ppermute | solution.py:10
  28.4 18.8 %collective-permute-start.4 = (f32[1,1,24,4096]{3,2,1,0:T(8,128)S(1)}, f32[1,1,24,4096]{3,2,1,0:T(8,128)S(1)}, u32[]{:S(2)}, u32[]{:S(2)}) collective-permute-start(f32[1,1,24,4096]{3,2,1,0:T(8,128)S(1)} %divide_multiply_fusion.2), channel_id=1, source_target_pairs={{4,0},{0,4},{5,1},{1,5},{6,2},{2,6},{7,3},{3,7},{12,8},{8,12},{13,... | collective-permute-start | bytes 1179656 | tf_op jit(solution)/shard_map/ppermute | solution.py:10
  35.9 32.7 %collective-permute-start.8 = (f32[1,1,24,4096]{3,2,1,0:T(8,128)S(1)}, f32[1,1,24,4096]{3,2,1,0:T(8,128)S(1)}, u32[]{:S(2)}, u32[]{:S(2)}) collective-permute-start(f32[1,1,24,4096]{3,2,1,0:T(8,128)S(1)} %divide_multiply_fusion.1), channel_id=1, source_target_pairs={{4,0},{0,4},{5,1},{1,5},{6,2},{2,6},{7,3},{3,7},{12,8},{8,12},{13,... | collective-permute-start | bytes 1179656 | tf_op jit(solution)/shard_map/ppermute | solution.py:10
where the time goes:
time: 70.6 us; the launch traced here: 70.3 us
  waiting for transfers between devices  25.5 us (36%)
  blocking collectives  19.9 us (28%)
  starting transfers between devices  13.4 us (19%)
  other arithmetic  5.57 us (8%)
  between operations  4.55 us (6%)
  local copies, waits for them, and re-layouts  1.53 us (2%)
    ppermute x12, waiting for transfers between devices, passed_along(): return lax.ppermute(block, axis, route)  25.5 us
    all_gather x1, blocking collectives, finish(): whole = lax.all_gather(rounded, 'fsdp', axis=2, tiled=True)  19.9 us
    ppermute x12, starting transfers between devices, passed_along(): return lax.ppermute(block, axis, route)  13.4 us
    mul x1, other arithmetic, row_round(): sent = (weight * states[0], weight * states[1], weight * states[2], weight)  2.33 us
    div x2, other arithmetic, col_round(): merged = tuple(((below[i] + sent[i] + above[i]) / total for i in range(3)))  1.59 us
    unnamed x3, local copies, waits for them, and re-layouts  1.53 us
  transfers between devices with their start and end apart: 12, of which 5 were waited for; matrix products, arithmetic and copies ran while one was open for 3% of the time, Pallas kernels for 0%

commit v1 on v0

v1 whole, which is shorter than its diff:
```python
import functools
import math
import jax
import jax.numpy as jnp
from jax import lax
from jax.experimental import pallas as pl
from jax.experimental.pallas import tpu as pltpu
from jax.sharding import PartitionSpec as P

LANES = 128
STEP = 4 * LANES
SCALE = 32767.0
DIGIT = 1024
COST = dict(c=4_000_000_000, a2=4_000_000_000, b2=4_000_000_000, d=4_000_000_000, a3=0, b3=4_000_000_000, v=0, m=0, ga=0, gb=10000000000, m4=4_000_000_000, pe=2_000_000_000, v4=0, pl=4_000_000_000, t1=2_000_000_000, t2=2_000_000_000, t3=4_000_000_000, gn=0)


def coded(x):
    size = jnp.minimum(jnp.maximum(jnp.abs(x), 1e-30), 16.0)
    root = lax.rsqrt(lax.rsqrt(size)) * (0.5 * SCALE)
    return jnp.round(jnp.where(x < 0, -root, root)).astype(jnp.int32).astype(jnp.int16)


def decoded(code):
    root = code.astype(jnp.int32).astype(jnp.float32) * (2.0 / SCALE)
    square = root * root
    return jnp.where(root < 0, -square, square) * square


def put_weight(ref, weight):
    whole = weight.astype(jnp.int32)
    lane = lax.broadcasted_iota(jnp.int32, whole.shape, 1)
    digits = jnp.where(lane < LANES // 2, lax.shift_right_logical(whole, 10), whole & (DIGIT - 1))
    ref[:, ref.shape[1] - LANES :] = digits.astype(jnp.int16)


def get_weight(ref):
    digits = ref[:, ref.shape[1] - LANES :].astype(jnp.int32).astype(jnp.float32)
    high = jnp.broadcast_to(digits[:, 0:1], digits.shape)
    low = jnp.broadcast_to(digits[:, LANES // 2 : LANES // 2 + 1], digits.shape)
    return high * float(DIGIT) + low


def over_lanes(columns, body):
    step = math.gcd(columns, STEP)

    @pl.loop(0, columns // step)
    def _(j):
        start = pl.multiple_of(j * step, step)
        for q in range(step // LANES):
            body(start + q * LANES)


def lanes(start, offset=0):
    return pl.ds(pl.multiple_of(start + offset, LANES), LANES)


def stepped(master, first, second, fix_first, fix_second):
    ratio = (first * fix_first) / (jnp.sqrt(second * fix_second) + 1e-08)
    return master - 0.1 * (ratio + 0.1 * master)


def first_of(moment_one, grad):
    return 0.9 * moment_one + 0.1 * grad


def second_of(moment_two, grad):
    return 0.95 * moment_two + 0.05 * grad * grad


def early_kernel(master, moment_one, moment_two, grads, counts, step, state, sent, weight_out, fixes, *refs):
    ins, (counts_in, sems) = refs[:4], refs[4:]
    part = state.shape[1]
    low = pl.ds(0, part)
    pairs = [(counts, counts_in)]
    pairs += [(a.at[:, low], b) for a, b in zip((moment_two, grads, moment_one, master), ins)]
    copies = [pltpu.make_async_copy(a, b, sems.at[i]) for i, (a, b) in enumerate(pairs)]
    for copy in copies:
        copy.start()
    copies[0].wait()
    shape = (master.shape[0], LANES)
    many = counts_in[...]
    lengths = lax.shift_left(jnp.ones_like(many), lax.broadcasted_iota(jnp.int32, many.shape, 1))
    total = jnp.sum((many * lengths).astype(jnp.float32), axis=1, keepdims=True)
    weight = jnp.broadcast_to(total, shape)
    weight_out[...] = weight
    put_weight(sent, weight)
    steps = jnp.full(shape, step[0].astype(jnp.float32))
    fix_first = 1.0 / (1.0 - jnp.exp(steps * math.log(0.9)))
    fix_second = 1.0 / (1.0 - jnp.exp(steps * math.log(0.95)))
    fixes[0] = fix_first
    fixes[1] = fix_second
    for copy in copies[1:]:
        copy.wait()
    second_in, grads_in, first_in, master_in = ins

    def body(start):
        at = lanes(start)
        grad = grads_in[:, at].astype(jnp.float32)
        first = first_of(first_in[:, at], grad)
        second = second_of(second_in[:, at], grad)
        new = stepped(master_in[:, at], first, second, fix_first, fix_second)
        state[:, at] = new
        sent[:, at] = coded(new)

    over_lanes(part, body)


def late_kernel(master, moment_one, moment_two, grads, weight, fixes, state, sent):
    part = state.shape[1]
    before = master.shape[1] - part
    put_weight(sent, weight[...])
    fix_first, fix_second = fixes[0], fixes[1]

    def body(start):
        at, high = lanes(start), lanes(start, before)
        grad = grads[:, high].astype(jnp.float32)
        first = first_of(moment_one[:, high], grad)
        second = second_of(moment_two[:, high], grad)
        new = stepped(master[:, high], first, second, fix_first, fix_second)
        state[:, at] = new
        sent[:, at] = coded(new)

    over_lanes(part, body)


def moment_kernel(formula, moment, grads, weight, state, sent):
    put_weight(sent, weight[...])

    def body(start):
        at = lanes(start)
        new = formula(moment[:, at], grads[:, at].astype(jnp.float32))
        state[:, at] = new
        sent[:, at] = coded(new)

    over_lanes(moment.shape[1], body)


def merged(state, own, others, factors):
    weights = [get_weight(own)] + [factor * get_weight(other) for factor, other in zip(factors, others)]
    total = functools.reduce(lax.add, weights)
    shares = [weight / total for weight in weights]

    def at_lanes(at):
        result = shares[0] * state[:, at]
        for share, other in zip(shares[1:], others):
            result = result + share * decoded(other[:, at])
        return result

    return total, at_lanes


def between_kernel(factors, state, own, *refs):
    others, (result, *copies) = refs[: len(factors)], refs[len(factors) :]
    total, at_lanes = merged(state, own, others, factors)
    for sent in copies:
        put_weight(sent, total)

    def body(start):
        at = lanes(start)
        new = at_lanes(at)
        result[:, at] = new
        code = coded(new)
        for sent in copies:
            sent[:, at] = code

    over_lanes(state.shape[1], body)


def last_master_kernel(factors, state, own, *refs):
    others, (result, rounded) = refs[: len(factors)], refs[len(factors) :]
    _, at_lanes = merged(state, own, others, factors)

    def body(start):
        at = lanes(start)
        new = at_lanes(at)
        result[:, at] = new
        rounded[:, at] = new.astype(jnp.bfloat16)

    over_lanes(state.shape[1], body)


def last_late_kernel(factors, state, own, early_rounded, *refs):
    others, (result, rounded, both_rounded) = refs[: len(factors)], refs[len(factors) :]
    _, at_lanes = merged(state, own, others, factors)
    before = early_rounded.shape[1]

    def body(start):
        at, high = lanes(start), lanes(start, before)
        new = at_lanes(at)
        result[:, at] = new
        rounded[:, at] = new.astype(jnp.bfloat16)
        both_rounded[:, high] = new.astype(jnp.bfloat16)

    over_lanes(state.shape[1], body)

    def copy_body(start):
        both_rounded[:, lanes(start)] = early_rounded[:, lanes(start)]

    over_lanes(before, copy_body)


def started(pairs, sems, first=0):
    copies = [pltpu.make_async_copy(a, b, sems.at[first + i]) for i, (a, b) in enumerate(pairs)]
    for copy in copies:
        copy.start()
    return copies


def last_moment(state, own, others, factors, new, result, sems):
    _, at_lanes = merged(state, own, others, factors)
    part = new.shape[1] // 2
    copies = []
    for i in range(2):

        def body(start, base=i * part):
            at = lanes(start, base)
            result[:, at] = at_lanes(at)

        over_lanes(part, body)
        columns = pl.ds(i * part, part)
        copies += started([(result.at[:, columns], new.at[:, columns])], sems, i)
    return copies


def first_moment_kernel(factors, state, own, *refs):
    others, (new, done, result, sems) = refs[: len(factors)], refs[len(factors) :]
    done[...] = jnp.zeros_like(done)
    for copy in last_moment(state, own, others, factors, new, result, sems):
        copy.wait()


def placed(pieces, whole, parts, axis):
    me = lax.axis_index(axis)
    pairs = []
    for part, blocks in zip(parts, pieces):
        pairs += [(block, whole.at[lax.bitwise_xor(me, k), :, part]) for k, block in blocks.items()]
    return pairs


def place_kernel(axis, names, early, late, *refs):
    blocks, (whole, new_master, done, sems) = refs[:-4], refs[-4:]
    done[...] = jnp.zeros_like(done)
    low, high = pl.ds(0, early.shape[1]), pl.ds(early.shape[1], late.shape[1])
    pairs = [(early, new_master.at[:, low]), (late, new_master.at[:, high])]
    pairs += placed(grouped(names, blocks), whole, (pl.ds(0, whole.shape[2]), low, high), axis)
    for copy in started(pairs, sems):
        copy.wait()


def last_kernel(axis, names, factors, size, _, state, own, *refs):
    others, refs = refs[: len(factors)], refs[len(factors) :]
    blocks, (whole, new, result, sems, place_sems) = refs[:-5], refs[-5:]
    low = whole.shape[2] - size
    parts = (pl.ds(0, whole.shape[2]), pl.ds(0, low), pl.ds(low, size))
    copies = started(placed(grouped(names, blocks), whole, parts, axis), place_sems)
    copies += last_moment(state, own, others, factors, new, result, sems)
    for copy in copies:
        copy.wait()


def grouped(names, blocks):
    blocks = iter(blocks)
    return [{k: next(blocks) for k in ks} for ks in names]


def pass_kernel(*_):
    pass


VMEM = pl.BlockSpec(memory_space=pltpu.VMEM)
SMEM = pl.BlockSpec(memory_space=pltpu.SMEM)
HBM = pl.BlockSpec(memory_space=pltpu.HBM)
DONE = ((8, LANES), jnp.float32)


def local(kernel, outs, args, specs=None, out_specs=None, scratch=(), after=(), cost=0, aliases=None):
    specs = specs or [VMEM] * len(args)
    body, skipped = kernel, len(args)

    def ordered_kernel(*refs):
        body(*refs[:skipped], *refs[skipped + len(after) :])

    return pl.pallas_call(
        ordered_kernel if after else kernel,
        out_shape=[jax.ShapeDtypeStruct(shape, kind) for shape, kind in outs],
        in_specs=[*specs, *[pl.BlockSpec(memory_space=pl.ANY)] * len(after)],
        out_specs=out_specs or [VMEM] * len(outs),
        scratch_shapes=scratch,
        input_output_aliases=aliases or {},
        compiler_params=pltpu.CompilerParams(vmem_limit_bytes=24 * 2**20),
        cost_estimate=pl.CostEstimate(flops=cost, bytes_accessed=0, transcendentals=0),
    )(*args, *after)


def along(block, axis, partner):
    return lax.ppermute(block, axis, [(i, partner(i)) for i in range(lax.axis_size(axis))])


def neighbours(block, axis, again=None):
    n = lax.axis_size(axis)
    if n == 2:
        return (2.0,), (along(block, axis, lambda i: i ^ 1),)
    again = block if again is None else again
    if n % 2:
        return (1.0, 1.0), tuple(along(x, axis, lambda i, k=k: (i + k) % n) for k, x in ((1, block), (-1, again)))
    far = along(block, axis, lambda i: (i + 1 if i % 2 else i - 1) % n)
    near = along(again, axis, lambda i: i ^ 1)
    return (1.0, 1.0), (near, far)


def between(state, sent, axis, after=(), cost=0, copies=1):
    factors, others = neighbours(sent, axis)
    outs = [(state.shape, jnp.float32)] + [(sent.shape, jnp.int16)] * copies
    return local(functools.partial(between_kernel, factors), outs, (state, sent, *others), after=after, cost=cost)


def held_until(block, after, cost=0):
    space = [pl.BlockSpec(memory_space=pl.ANY)]
    (same,) = local(pass_kernel, [(block.shape, block.dtype)], [block], space, space, after=after, cost=cost, aliases={0: 0})
    return same


def token_kernel(token):
    token[...] = jnp.zeros_like(token)


def turn(after, cost):
    return local(token_kernel, [DONE], [], [], after=after, cost=cost)


def exchanged(held, axis, far):
    return {**held, **{k ^ far: along(block, axis, lambda i: i ^ far) for k, block in held.items()}}


def per_device(master, moment_one, moment_two, grads, counts, step):
    rows, columns = master.shape[2:]
    n = lax.axis_size("fsdp")
    f32, s16, bf16 = jnp.float32, jnp.int16, jnp.bfloat16
    own = [a.reshape(rows, columns) for a in (master, moment_one, moment_two, grads)]
    low = columns // 2 // LANES * LANES
    full, low_part, high_part = (rows, columns), (rows, low), (rows, columns - low)
    tile = (rows, LANES)

    def with_weight(shape):
        return ((rows, shape[1] + LANES), s16)

    early, sent_early, weight, fixes = local(
        early_kernel,
        [(low_part, f32), with_weight(low_part), (tile, f32), ((2, *tile), f32)],
        [*[pltpu.with_memory_space_constraint(a, pltpu.HBM) for a in (*own, counts.reshape(1, -1))], step],
        [HBM] * 5 + [SMEM],
        scratch=[
            pltpu.VMEM(low_part, f32),
            pltpu.VMEM(low_part, bf16),
            pltpu.VMEM(low_part, f32),
            pltpu.VMEM(low_part, f32),
            pltpu.VMEM((1, counts.shape[2]), jnp.int32),
            pltpu.SemaphoreType.DMA((5,)),
        ],
    )
    late, sent_late = local(
        late_kernel, [(high_part, f32), with_weight(high_part)], [*own, weight, fixes], after=[sent_early]
    )
    first, sent_first = local(
        functools.partial(moment_kernel, first_of),
        [(full, f32), with_weight(full)],
        [own[1], own[3], weight],
        after=[sent_late],
        cost=COST["c"],
    )
    early, sent_early = between(early, sent_early, "row", after=[sent_first], cost=COST["a2"])
    late, sent_late = between(late, sent_late, "row", after=[sent_early], cost=COST["b2"])
    second, sent_second = local(
        functools.partial(moment_kernel, second_of),
        [(full, f32), with_weight(full)],
        [own[2], own[3], weight],
        after=[sent_late],
        cost=COST["d"],
    )

    factors, others = neighbours(sent_early, "col")
    early, rounded_early = local(
        functools.partial(last_master_kernel, factors),
        [(low_part, f32), (low_part, bf16)],
        (early, sent_early, *others),
        after=[sent_second],
        cost=COST["a3"],
    )
    factors, others = neighbours(sent_late, "col")
    late, rounded_late, rounded = local(
        functools.partial(last_late_kernel, factors),
        [(high_part, f32), (high_part, bf16), (full, bf16)],
        (late, sent_late, rounded_early, *others),
        cost=COST["b3"],
    )
    halves = [{0: rounded_early}, {0: rounded_late}]
    far = n // 2
    while far > 1:
        halves = [exchanged(held, "fsdp", far) for held in halves]
        far //= 2
    wholes = exchanged({0: rounded}, "fsdp", 1)

    first, sent_first = between(first, sent_first, "row", after=[rounded], cost=COST["m"])
    second, sent_second, again = between(second, sent_second, "col", after=[sent_first], cost=COST["v"], copies=2)
    halves = [{k: block for k, block in held.items() if k} for held in halves]
    halves[0] = {k: held_until(block, turn([sent_second], COST["t1"]), COST["ga"]) for k, block in halves[0].items()}
    halves[1] = {k: held_until(block, turn(list(halves[0].values()), COST["t2"]), COST["gb"]) for k, block in halves[1].items()}
    again = held_until(again, list(halves[1].values()), COST["gn"])
    halves = [exchanged(held, "fsdp", 1) for held in halves]

    factors, others = neighbours(sent_first, "col")
    new_first, done = local(
        functools.partial(first_moment_kernel, factors),
        [(full, f32), DONE],
        (first, sent_first, *others),
        out_specs=[HBM, VMEM],
        scratch=[pltpu.VMEM(full, f32), pltpu.SemaphoreType.DMA((2,))],
        after=[halves[1][2]],
        cost=COST["m4"],
    )
    sooner = ((0, 1), tuple(range(2, n)), tuple(range(2, n, 2)))
    later = ((), (), tuple(range(3, n, 2)))
    groups = (wholes, *halves)
    blocks = [group[k] for ks, group in zip(sooner, groups) for k in ks]
    whole, new_master, done = local(
        functools.partial(place_kernel, "fsdp", sooner),
        [((n, rows, columns), bf16), (full, f32), DONE],
        (early, late, *blocks),
        out_specs=[HBM, HBM, VMEM],
        scratch=[pltpu.SemaphoreType.DMA((2 + len(blocks),))],
        after=[done],
        cost=COST["pe"],
    )
    factors, others = neighbours(sent_second, "row", again)
    blocks = [group[k] for ks, group in zip(later, groups) for k in ks]
    whole, new_second = local(
        functools.partial(last_kernel, "fsdp", later, factors, columns - low),
        [((n, rows, columns), bf16), (full, f32)],
        (whole, second, sent_second, *others, *blocks),
        [HBM] + [VMEM] * (2 + len(others) + len(blocks)),
        [HBM, HBM],
        scratch=[pltpu.VMEM(full, f32), pltpu.SemaphoreType.DMA((2,)), pltpu.SemaphoreType.DMA((len(blocks),))],
        after=turn([done, *blocks], COST["t3"]),
        cost=COST["v4"],
        aliases={0: 0},
    )
    parts = [a.reshape(master.shape) for a in (new_master, new_first, new_second)]
    return (*parts, whole.reshape(1, 1, 1, n * rows, columns))


def solution(mesh):
    sharded = P("row", "col", "fsdp", None)
    return jax.shard_map(
        per_device,
        mesh=mesh,
        in_specs=(sharded, sharded, sharded, sharded, P("row", "col", None), P()),
        out_specs=(sharded, sharded, sharded, P("row", "col", "fsdp", None, None)),
        check_vma=False,
    )
```

time: 70.6 us -> 34.3 us (0.49)
  waiting for transfers between devices: 25.5 us -> 4.67 us
  blocking collectives: 19.9 us -> 0 us
  Pallas kernels: 0 us -> 8.1 us
  starting transfers between devices: 13.4 us -> 19.9 us
  other arithmetic: 5.57 us -> 0 us
  between operations: 4.55 us -> 1.47 us
  local copies, waits for them, and re-layouts: 1.53 us -> 0.02 us
    ppermute x12 -> x17, waiting for transfers between devices: 25.5 us -> 4.67 us  [along(): lax.ppermute(block, axis, [(i, partner(i)) for i in range(lax.axis_size(a...]
    all_gather x1 -> x0, blocking collectives: 19.9 us -> none  [finish(): whole = lax.all_gather(rounded, 'fsdp', axis=2, tiled=True)]
    pallas_call x0 -> x19, Pallas kernels: none -> 8.1 us  [local(): pl.pallas_call(ordered_kernel if after else kernel, out_shape=[jax.ShapeD...]
    ppermute x12 -> x17, starting transfers between devices: 13.4 us -> 19.9 us  [along(): lax.ppermute(block, axis, [(i, partner(i)) for i in range(lax.axis_size(a...]
    mul x4 -> x0, other arithmetic: 2.57 us -> none  [the longest x1 2.33 us: row_round(): sent = (weight * states[0], weight * states[1], weight * states[2], weight)]
    div x2 -> x0, other arithmetic: 1.59 us -> none  [col_round(): merged = tuple(((below[i] + sent[i] + above[i]) / total for i in range(3)))]
    unnamed x3 -> x8, local copies, waits for them, and re-layouts: 1.53 us -> 0.02 us
    convert_element_type x1 -> x0, other arithmetic: 0.8 us -> none  [finish(): rounded = after_col[0].astype(jnp.bfloat16)]
  transfers between devices with their start and end apart: 12 -> 17, of which waited for: 5 -> 6; matrix products, arithmetic and copies ran while one was open for 3% -> 0% of each run, Pallas kernels for 0% -> 16%
where the time goes in v1:
time: 34.3 us; the launch traced here: 34.2 us
  starting transfers between devices  19.9 us (58%)
  Pallas kernels  8.1 us (24%)
  waiting for transfers between devices  4.67 us (14%)
  between operations  1.47 us (4%)
    ppermute x17, starting transfers between devices, along(): lax.ppermute(block, axis, [(i, partner(i)) for i in range(lax.axis_size(a...  19.9 us
    pallas_call x19, Pallas kernels, local(): pl.pallas_call(ordered_kernel if after else kernel, out_shape=[jax.ShapeD...  8.1 us
    ppermute x17, waiting for transfers between devices, along(): lax.ppermute(block, axis, [(i, partner(i)) for i in range(lax.axis_size(a...  4.67 us
  transfers between devices with their start and end apart: 17, of which 6 were waited for; matrix products, arithmetic and copies ran while one was open for 0% of the time, Pallas kernels for 16%

profile of v1, /device:TPU:0, one launch (start us, length us, event | category | flops | bytes accessed | tf_op | source)
XLA Modules:
  0.0 34.2 jit_solution(11050567484282928397)
XLA Ops:
  1.3 0.0 copy-start
  1.3 1.6 %shard_map.93 = (f32[24,2048]{1,0:T(8,128)S(1)}, s16[24,2176]{1,0:T(8,128)(2,1)S(1)}, f32[24,128]{1,0:T(8,128)S(1)}, f32[2,24,128]{2,1,0:T(8,128)S(1)}) custom-call(f32[24,4096]{1,0:T(8,128)} %bitcast.9, f32[24,4096]{1,0:T(8,128)} %bitcast.11, f32[24,4096]{1,0:T(8,128)} %bitcast.14, bf16[24,4096]{1,0:T(8,128)(2,1)} %bitcast.17, s32[1,8]{1,0:T(1,128)} %bitcast.22, ...), custom_call_target="tpu_custom_call" | custom-call | tf_op jit(solution)/shard_map/pallas_call | solution.py:283
  3.0 2.5 %collective-permute-start.1 = (s16[24,2176]{1,0:T(8,128)(2,1)S(1)}, s16[24,2176]{1,0:T(8,128)(2,1)S(1)}, u32[]{:S(2)}, u32[]{:S(2)}) collective-permute-start(s16[24,2176]{1,0:T(8,128)(2,1)S(1)} %get-tuple-element.36.refs_6_.refs_1_), channel_id=1, source_target_pairs={{0,24},{8,16},{16,8},{24,0},{1,25},{9,17},{17,9},{25,1},{2,26},{10... | collective-permute-start | bytes 313352 | tf_op jit(solution)/shard_map/ppermute | solution.py:296
  5.4 0.7 %collective-permute-start = (s16[24,2176]{1,0:T(8,128)(2,1)S(1)}, s16[24,2176]{1,0:T(8,128)(2,1)S(1)}, u32[]{:S(2)}, u32[]{:S(2)}) collective-permute-start(s16[24,2176]{1,0:T(8,128)(2,1)S(1)} %get-tuple-element.36.refs_6_.refs_1_), channel_id=1, source_target_pairs={{0,8},{8,0},{16,24},{24,16},{1,9},{9,1},{17,25},{25,17},{2,10},{10... | collective-permute-start | bytes 313352 | tf_op jit(solution)/shard_map/ppermute | solution.py:296
  6.1 0.3 shard_map.94
  6.5 0.1 collective-permute-start.4
  6.6 0.0 collective-permute-start.3
  6.6 0.4 %shard_map.95 = (f32[24,4096]{1,0:T(8,128)S(1)}, s16[24,4224]{1,0:T(8,128)(2,1)S(1)}) custom-call(f32[24,4096]{1,0:T(8,128)S(1)} %bitcast.13, bf16[24,4096]{1,0:T(8,128)(2,1)S(1)} %bitcast.19, f32[24,128]{1,0:T(8,128)S(1)} %get-tuple-element.37.refs_4_.refs_2_, s16[24,2176]{1,0:T(8,128)(2,1)S(1)} %get-tuple-element.39.refs_3_.refs_1_), custom_call_target="tpu_custom_call" | custom-call | flops 4000000000 | tf_op jit(solution)/shard_map/pallas_call | solution.py:283
  7.0 1.7 %collective-permute-start.10 = (s16[24,4224]{1,0:T(8,128)(2,1)S(1)}, s16[24,4224]{1,0:T(8,128)(2,1)S(1)}, u32[]{:S(2)}, u32[]{:S(2)}) collective-permute-start(s16[24,4224]{1,0:T(8,128)(2,1)S(1)} %get-tuple-element.40.refs_4_.refs_1_), channel_id=1, source_target_pairs={{0,24},{8,16},{16,8},{24,0},{1,25},{9,17},{17,9},{25,1},{2,26},{10... | collective-permute-start | bytes 608264 | tf_op jit(solution)/shard_map/ppermute | solution.py:296
  8.7 0.1 collective-permute-done.1.refs_3_
  8.8 0.4 %collective-permute-start.9 = (s16[24,4224]{1,0:T(8,128)(2,1)S(1)}, s16[24,4224]{1,0:T(8,128)(2,1)S(1)}, u32[]{:S(2)}, u32[]{:S(2)}) collective-permute-start(s16[24,4224]{1,0:T(8,128)(2,1)S(1)} %get-tuple-element.40.refs_4_.refs_1_), channel_id=1, source_target_pairs={{0,8},{8,0},{16,24},{24,16},{1,9},{9,1},{17,25},{25,17},{2,10},{10... | collective-permute-start | bytes 608264 | tf_op jit(solution)/shard_map/ppermute | solution.py:296
  9.2 0.0 collective-permute-done.refs_2_
  9.2 0.4 %shard_map.96 = (f32[24,2048]{1,0:T(8,128)S(1)}, s16[24,2176]{1,0:T(8,128)(2,1)S(1)}) custom-call(f32[24,2048]{1,0:T(8,128)S(1)} %get-tuple-element.35.refs_0_, s16[24,2176]{1,0:T(8,128)(2,1)S(1)} %get-tuple-element.36.refs_6_.refs_1_, s16[24,2176]{1,0:T(8,128)(2,1)S(1)} %collective-permute-done.refs_2_, s16[24,2176]{1,0:T(8,128)(2,1)S(1)} %collective-permute-done.1.refs_3_, ...), custom_call_target="tpu_custom_call" | custom-call | flops 4000000000 | tf_op jit(solution)/shard_map/pallas_call | solution.py:283
  9.6 2.2 %collective-permute-start.2 = (s16[24,2176]{1,0:T(8,128)(2,1)S(1)}, s16[24,2176]{1,0:T(8,128)(2,1)S(1)}, u32[]{:S(2)}, u32[]{:S(2)}) collective-permute-start(s16[24,2176]{1,0:T(8,128)(2,1)S(1)} %get-tuple-element.42.refs_4_.refs_1_), channel_id=1, source_target_pairs={{0,4},{4,0},{1,5},{5,1},{2,6},{6,2},{3,7},{7,3},{8,12},{12,8},{9,1... | collective-permute-start | bytes 313352 | tf_op jit(solution)/shard_map/ppermute | solution.py:296
  11.8 0.0 collective-permute-done.4.refs_3_
  11.8 0.0 collective-permute-done.3.refs_2_
  11.8 0.4 %shard_map.97 = (f32[24,2048]{1,0:T(8,128)S(1)}, s16[24,2176]{1,0:T(8,128)(2,1)S(1)}) custom-call(f32[24,2048]{1,0:T(8,128)S(1)} %get-tuple-element.43.refs_0_, s16[24,2176]{1,0:T(8,128)(2,1)S(1)} %get-tuple-element.39.refs_3_.refs_1_, s16[24,2176]{1,0:T(8,128)(2,1)S(1)} %collective-permute-done.3.refs_2_, ...), custom_call_target="tpu_custom_call" | custom-call | flops 4000000000 | tf_op jit(solution)/shard_map/pallas_call | solution.py:283
  12.2 1.6 %collective-permute-start.5 = (s16[24,2176]{1,0:T(8,128)(2,1)S(1)}, s16[24,2176]{1,0:T(8,128)(2,1)S(1)}, u32[]{:S(2)}, u32[]{:S(2)}) collective-permute-start(s16[24,2176]{1,0:T(8,128)(2,1)S(1)} %get-tuple-element.44.refs_3_.own), channel_id=1, source_target_pairs={{0,4},{4,0},{1,5},{5,1},{2,6},{6,2},{3,7},{7,3},{8,12},{12,8},{9,1... | collective-permute-start | bytes 313352 | tf_op jit(solution)/shard_map/ppermute | solution.py:296
  13.8 0.4 %shard_map.98 = (f32[24,4096]{1,0:T(8,128)S(1)}, s16[24,4224]{1,0:T(8,128)(2,1)S(1)}) custom-call(f32[24,4096]{1,0:T(8,128)S(1)} %bitcast.16, bf16[24,4096]{1,0:T(8,128)(2,1)S(1)} %bitcast.20, f32[24,128]{1,0:T(8,128)S(1)} %get-tuple-element.37.refs_4_.refs_2_, s16[24,2176]{1,0:T(8,128)(2,1)S(1)} %get-tuple-element.44.refs_3_.own), custom_call_target="tpu_custom_call" | custom-call | flops 4000000000 | tf_op jit(solution)/shard_map/pallas_call | solution.py:283
  14.2 0.6 %collective-permute-start.8 = (s16[24,4224]{1,0:T(8,128)(2,1)S(1)}, s16[24,4224]{1,0:T(8,128)(2,1)S(1)}, u32[]{:S(2)}, u32[]{:S(2)}) collective-permute-start(s16[24,4224]{1,0:T(8,128)(2,1)S(1)} %get-tuple-element.45.refs_3_.refs_1_), channel_id=1, source_target_pairs={{0,4},{4,0},{1,5},{5,1},{2,6},{6,2},{3,7},{7,3},{8,12},{12,8},{9,1... | collective-permute-start | bytes 608264 | tf_op jit(solution)/shard_map/ppermute | solution.py:296
  14.7 0.4 %collective-permute-done.2.refs_2_ = s16[24,2176]{1,0:T(8,128)(2,1)S(1)} collective-permute-done((s16[24,2176]{1,0:T(8,128)(2,1)S(1)}, s16[24,2176]{1,0:T(8,128)(2,1)S(1)}, u32[]{:S(2)}, u32[]{:S(2)}) %collective-permute-start.2) | collective-permute-done | bytes 104480 | tf_op jit(solution)/shard_map/ppermute | solution.py:296
  15.2 0.2 shard_map.99
  15.4 3.1 %collective-permute-start.7 = (bf16[24,2048]{1,0:T(8,128)(2,1)S(1)}, bf16[24,2048]{1,0:T(8,128)(2,1)S(1)}, u32[]{:S(2)}, u32[]{:S(2)}) collective-permute-start(bf16[24,2048]{1,0:T(8,128)(2,1)S(1)} %get-tuple-element.48.early_rounded), channel_id=1, source_target_pairs={{0,2},{1,3},{2,0},{3,1},{4,6},{5,7},{6,4},{7,5},{8,10},{9,11},{10,... | collective-permute-start | bytes 294920 | tf_op jit(solution)/shard_map/ppermute | solution.py:296
  18.5 0.0 collective-permute-done.5.refs_0_
  18.5 0.2 shard_map.100
  18.7 2.2 %collective-permute-start.12 = (bf16[24,2048]{1,0:T(8,128)(2,1)S(1)}, bf16[24,2048]{1,0:T(8,128)(2,1)S(1)}, u32[]{:S(2)}, u32[]{:S(2)}) collective-permute-start(bf16[24,2048]{1,0:T(8,128)(2,1)S(1)} %get-tuple-element.55), channel_id=1, source_target_pairs={{0,2},{1,3},{2,0},{3,1},{4,6},{5,7},{6,4},{7,5},{8,10},{9,11},{10,... | collective-permute-start | bytes 294920 | tf_op jit(solution)/shard_map/ppermute | solution.py:296
  21.0 0.0 collective-permute-done.10.refs_3_
  21.0 1.6 %collective-permute-start.6 = (bf16[24,4096]{1,0:T(8,128)(2,1)S(1)}, bf16[24,4096]{1,0:T(8,128)(2,1)S(1)}, u32[]{:S(2)}, u32[]{:S(2)}) collective-permute-start(bf16[24,4096]{1,0:T(8,128)(2,1)S(1)} %get-tuple-element.50.refs_4_.refs_2_), channel_id=1, source_target_pairs={{0,1},{1,0},{2,3},{3,2},{4,5},{5,4},{6,7},{7,6},{8,9},{9,8},{10,11... | collective-permute-start | bytes 589832 | tf_op jit(solution)/shard_map/ppermute | solution.py:296
  22.5 0.0 collective-permute-done.9.refs_2_
  22.5 0.6 %shard_map.101 = (f32[24,4096]{1,0:T(8,128)S(1)}, s16[24,4224]{1,0:T(8,128)(2,1)S(1)}) custom-call(f32[24,4096]{1,0:T(8,128)S(1)} %get-tuple-element.52.refs_0_, s16[24,4224]{1,0:T(8,128)(2,1)S(1)} %get-tuple-element.40.refs_4_.refs_1_, s16[24,4224]{1,0:T(8,128)(2,1)S(1)} %collective-permute-done.9.refs_2_, ...), custom_call_target="tpu_custom_call" | custom-call | tf_op jit(solution)/shard_map/pallas_call | solution.py:283
  23.2 1.6 %collective-permute-start.13 = (s16[24,4224]{1,0:T(8,128)(2,1)S(1)}, s16[24,4224]{1,0:T(8,128)(2,1)S(1)}, u32[]{:S(2)}, u32[]{:S(2)}) collective-permute-start(s16[24,4224]{1,0:T(8,128)(2,1)S(1)} %get-tuple-element.53.refs_3_.refs_1_), channel_id=1, source_target_pairs={{0,4},{4,0},{1,5},{5,1},{2,6},{6,2},{3,7},{7,3},{8,12},{12,8},{9,1... | collective-permute-start | bytes 608264 | tf_op jit(solution)/shard_map/ppermute | solution.py:296
  24.7 0.0 collective-permute-done.8.refs_2_
  24.7 0.5 %shard_map.102 = (f32[24,4096]{1,0:T(8,128)S(1)}, s16[24,4224]{1,0:T(8,128)(2,1)S(1)}, s16[24,4224]{1,0:T(8,128)(2,1)S(1)}) custom-call(f32[24,4096]{1,0:T(8,128)S(1)} %get-tuple-element.51.refs_0_, s16[24,4224]{1,0:T(8,128)(2,1)S(1)} %get-tuple-element.45.refs_3_.refs_1_, s16[24,4224]{1,0:T(8,128)(2,1)S(1)} %collective-permute-done.8.refs_2_, ...), custom_call_target="tpu_custom_call" | custom-call | tf_op jit(solution)/shard_map/pallas_call | solution.py:283
  25.3 0.1 collective-permute-start.15
  25.3 0.0 collective-permute-done.7.refs_0_
  25.4 0.9 %collective-permute-start.11 = (bf16[24,2048]{1,0:T(8,128)(2,1)S(1)}, bf16[24,2048]{1,0:T(8,128)(2,1)S(1)}, u32[]{:S(2)}, u32[]{:S(2)}) collective-permute-start(bf16[24,2048]{1,0:T(8,128)(2,1)S(1)} %shard_map.104.refs_0_.refs_4_), channel_id=1, source_target_pairs={{0,1},{1,0},{2,3},{3,2},{4,5},{5,4},{6,7},{7,6},{8,9},{9,8},{10,11... | collective-permute-start | bytes 294920 | tf_op jit(solution)/shard_map/ppermute | solution.py:296
  26.3 0.8 %collective-permute-done.12.refs_0_ = bf16[24,2048]{1,0:T(8,128)(2,1)S(1)} collective-permute-done((bf16[24,2048]{1,0:T(8,128)(2,1)S(1)}, bf16[24,2048]{1,0:T(8,128)(2,1)S(1)}, u32[]{:S(2)}, u32[]{:S(2)}) %collective-permute-start.12) | collective-permute-done | bytes 98336 | tf_op jit(solution)/shard_map/ppermute | solution.py:296
  27.2 0.5 %collective-permute-start.16 = (bf16[24,2048]{1,0:T(8,128)(2,1)S(1)}, bf16[24,2048]{1,0:T(8,128)(2,1)S(1)}, u32[]{:S(2)}, u32[]{:S(2)}) collective-permute-start(bf16[24,2048]{1,0:T(8,128)(2,1)S(1)} %shard_map.106.refs_3_.refs_6_.refs_1_), channel_id=1, source_target_pairs={{0,1},{1,0},{2,3},{3,2},{4,5},{5,4},{6,7},{7,6},{8,9},{9,8},{10,11... | collective-permute-start | bytes 294920 | tf_op jit(solution)/shard_map/ppermute | solution.py:296
  27.7 1.3 %collective-permute-done.13.refs_2_ = s16[24,4224]{1,0:T(8,128)(2,1)S(1)} collective-permute-done((s16[24,4224]{1,0:T(8,128)(2,1)S(1)}, s16[24,4224]{1,0:T(8,128)(2,1)S(1)}, u32[]{:S(2)}, u32[]{:S(2)}) %collective-permute-start.13) | collective-permute-done | bytes 202784 | tf_op jit(solution)/shard_map/ppermute | solution.py:296
  29.0 0.0 collective-permute-start.14
  29.0 1.0 %shard_map.107 = (f32[24,4096]{1,0:T(8,128)}, f32[8,128]{1,0:T(8,128)S(1)}) custom-call(f32[24,4096]{1,0:T(8,128)S(1)} %get-tuple-element.56.refs_0_, s16[24,4224]{1,0:T(8,128)(2,1)S(1)} %get-tuple-element.53.refs_3_.refs_1_, s16[24,4224]{1,0:T(8,128)(2,1)S(1)} %collective-permute-done.13.refs_2_, bf16[24,2048]{1,0:T(8,128)(2,1)S(1)} %shard_map.106.refs_3_.refs_6_.refs_1_), custom_call_target="tpu_custom_call" | custom-call | flops 4000000000 | tf_op jit(solution)/shard_map/pallas_call | solution.py:283
  30.0 0.0 collective-permute-done.6.refs_3_
  30.0 0.9 %collective-permute-done.11.refs_5_ = bf16[24,2048]{1,0:T(8,128)(2,1)S(1)} collective-permute-done((bf16[24,2048]{1,0:T(8,128)(2,1)S(1)}, bf16[24,2048]{1,0:T(8,128)(2,1)S(1)}, u32[]{:S(2)}, u32[]{:S(2)}) %collective-permute-start.11) | collective-permute-done | bytes 98336 | tf_op jit(solution)/shard_map/ppermute | solution.py:296
  30.9 1.0 %shard_map.108 = (bf16[4,24,4096]{2,1,0:T(8,128)(2,1)}, f32[24,4096]{1,0:T(8,128)}, f32[8,128]{1,0:T(8,128)S(1)}) custom-call(f32[24,2048]{1,0:T(8,128)S(1)} %get-tuple-element.46.refs_0_, f32[24,2048]{1,0:T(8,128)S(1)} %get-tuple-element.49.refs_1_, bf16[24,4096]{1,0:T(8,128)(2,1)S(1)} %get-tuple-element.50.refs_4_.refs_2_, ...), custom_call_target="tpu_custom_call" | custom-call | flops 2000000000 | tf_op jit(solution)/shard_map/pallas_call | solution.py:283
  32.0 1.1 %collective-permute-done.16.refs_1_.refs_5_ = bf16[24,2048]{1,0:T(8,128)(2,1)S(1)} collective-permute-done((bf16[24,2048]{1,0:T(8,128)(2,1)S(1)}, bf16[24,2048]{1,0:T(8,128)(2,1)S(1)}, u32[]{:S(2)}, u32[]{:S(2)}) %collective-permute-start.16) | collective-permute-done | bytes 98336 | tf_op jit(solution)/shard_map/ppermute | solution.py:296
  33.0 0.0 collective-permute-done.14.refs_3_
  33.0 0.0 collective-permute-done.15.refs_4_
  33.0 1.1 %shard_map.111 = (bf16[4,24,4096]{2,1,0:T(8,128)(2,1)}, f32[24,4096]{1,0:T(8,128)}) custom-call(bf16[4,24,4096]{2,1,0:T(8,128)(2,1)} %get-tuple-element.60.refs_0_, f32[24,4096]{1,0:T(8,128)S(1)} %get-tuple-element.61.refs_1_, s16[24,4224]{1,0:T(8,128)(2,1)S(1)} %get-tuple-element.54.refs_0_.refs_2_, ...), custom_call_target="tpu_custom_call", output_to_operand_aliasing={{0}: (0, {})} | custom-call | tf_op jit(solution)/shard_map/pallas_call | solution.py:283
  (13 shorter events, 0.0 us)
Async XLA Ops:
  1.3 4.8 %copy-start = (f32[1,1,24,4096]{3,2,1,0:T(8,128)S(1)}, f32[1,1,24,4096]{3,2,1,0:T(8,128)}, u32[]{:S(2)}) copy-start(f32[1,1,24,4096]{3,2,1,0:T(8,128)} %param.6) | copy-start | bytes 1179652
  1.3 4.8 %copy-start.1 = (f32[1,1,24,4096]{3,2,1,0:T(8,128)S(1)}, f32[1,1,24,4096]{3,2,1,0:T(8,128)}, u32[]{:S(2)}) copy-start(f32[1,1,24,4096]{3,2,1,0:T(8,128)} %param.7) | copy-start | bytes 1179652
  1.3 4.8 %copy-start.2 = (f32[1,1,24,4096]{3,2,1,0:T(8,128)S(1)}, f32[1,1,24,4096]{3,2,1,0:T(8,128)}, u32[]{:S(2)}) copy-start(f32[1,1,24,4096]{3,2,1,0:T(8,128)} %param.8) | copy-start | bytes 1179652
  1.3 4.8 %copy-start.3 = (bf16[1,1,24,4096]{3,2,1,0:T(8,128)(2,1)S(1)}, bf16[1,1,24,4096]{3,2,1,0:T(8,128)(2,1)}, u32[]{:S(2)}) copy-start(bf16[1,1,24,4096]{3,2,1,0:T(8,128)(2,1)} %param.9) | copy-start | bytes 589828
  3.0 5.8 %collective-permute-start.1 = (s16[24,2176]{1,0:T(8,128)(2,1)S(1)}, s16[24,2176]{1,0:T(8,128)(2,1)S(1)}, u32[]{:S(2)}, u32[]{:S(2)}) collective-permute-start(s16[24,2176]{1,0:T(8,128)(2,1)S(1)} %get-tuple-element.36.refs_6_.refs_1_), channel_id=1, source_target_pairs={{0,24},{8,16},{16,8},{24,0},{1,25},{9,17},{17,9},{25,1},{2,26},{10... | collective-permute-start | bytes 313352 | tf_op jit(solution)/shard_map/ppermute | solution.py:296
  5.4 3.8 %collective-permute-start = (s16[24,2176]{1,0:T(8,128)(2,1)S(1)}, s16[24,2176]{1,0:T(8,128)(2,1)S(1)}, u32[]{:S(2)}, u32[]{:S(2)}) collective-permute-start(s16[24,2176]{1,0:T(8,128)(2,1)S(1)} %get-tuple-element.36.refs_6_.refs_1_), channel_id=1, source_target_pairs={{0,8},{8,0},{16,24},{24,16},{1,9},{9,1},{17,25},{25,17},{2,10},{10... | collective-permute-start | bytes 313352 | tf_op jit(solution)/shard_map/ppermute | solution.py:296
  6.5 5.4 %collective-permute-start.4 = (s16[24,2176]{1,0:T(8,128)(2,1)S(1)}, s16[24,2176]{1,0:T(8,128)(2,1)S(1)}, u32[]{:S(2)}, u32[]{:S(2)}) collective-permute-start(s16[24,2176]{1,0:T(8,128)(2,1)S(1)} %get-tuple-element.39.refs_3_.refs_1_), channel_id=1, source_target_pairs={{0,24},{8,16},{16,8},{24,0},{1,25},{9,17},{17,9},{25,1},{2,26},{10... | collective-permute-start | bytes 313352 | tf_op jit(solution)/shard_map/ppermute | solution.py:296
  6.6 5.2 %collective-permute-start.3 = (s16[24,2176]{1,0:T(8,128)(2,1)S(1)}, s16[24,2176]{1,0:T(8,128)(2,1)S(1)}, u32[]{:S(2)}, u32[]{:S(2)}) collective-permute-start(s16[24,2176]{1,0:T(8,128)(2,1)S(1)} %get-tuple-element.39.refs_3_.refs_1_), channel_id=1, source_target_pairs={{0,8},{8,0},{16,24},{24,16},{1,9},{9,1},{17,25},{25,17},{2,10},{10... | collective-permute-start | bytes 313352 | tf_op jit(solution)/shard_map/ppermute | solution.py:296
  7.0 14.0 %collective-permute-start.10 = (s16[24,4224]{1,0:T(8,128)(2,1)S(1)}, s16[24,4224]{1,0:T(8,128)(2,1)S(1)}, u32[]{:S(2)}, u32[]{:S(2)}) collective-permute-start(s16[24,4224]{1,0:T(8,128)(2,1)S(1)} %get-tuple-element.40.refs_4_.refs_1_), channel_id=1, source_target_pairs={{0,24},{8,16},{16,8},{24,0},{1,25},{9,17},{17,9},{25,1},{2,26},{10... | collective-permute-start | bytes 608264 | tf_op jit(solution)/shard_map/ppermute | solution.py:296
  8.8 13.8 %collective-permute-start.9 = (s16[24,4224]{1,0:T(8,128)(2,1)S(1)}, s16[24,4224]{1,0:T(8,128)(2,1)S(1)}, u32[]{:S(2)}, u32[]{:S(2)}) collective-permute-start(s16[24,4224]{1,0:T(8,128)(2,1)S(1)} %get-tuple-element.40.refs_4_.refs_1_), channel_id=1, source_target_pairs={{0,8},{8,0},{16,24},{24,16},{1,9},{9,1},{17,25},{25,17},{2,10},{10... | collective-permute-start | bytes 608264 | tf_op jit(solution)/shard_map/ppermute | solution.py:296
  9.6 5.6 %collective-permute-start.2 = (s16[24,2176]{1,0:T(8,128)(2,1)S(1)}, s16[24,2176]{1,0:T(8,128)(2,1)S(1)}, u32[]{:S(2)}, u32[]{:S(2)}) collective-permute-start(s16[24,2176]{1,0:T(8,128)(2,1)S(1)} %get-tuple-element.42.refs_4_.refs_1_), channel_id=1, source_target_pairs={{0,4},{4,0},{1,5},{5,1},{2,6},{6,2},{3,7},{7,3},{8,12},{12,8},{9,1... | collective-permute-start | bytes 313352 | tf_op jit(solution)/shard_map/ppermute | solution.py:296
  12.2 6.3 %collective-permute-start.5 = (s16[24,2176]{1,0:T(8,128)(2,1)S(1)}, s16[24,2176]{1,0:T(8,128)(2,1)S(1)}, u32[]{:S(2)}, u32[]{:S(2)}) collective-permute-start(s16[24,2176]{1,0:T(8,128)(2,1)S(1)} %get-tuple-element.44.refs_3_.own), channel_id=1, source_target_pairs={{0,4},{4,0},{1,5},{5,1},{2,6},{6,2},{3,7},{7,3},{8,12},{12,8},{9,1... | collective-permute-start | bytes 313352 | tf_op jit(solution)/shard_map/ppermute | solution.py:296
  14.2 10.6 %collective-permute-start.8 = (s16[24,4224]{1,0:T(8,128)(2,1)S(1)}, s16[24,4224]{1,0:T(8,128)(2,1)S(1)}, u32[]{:S(2)}, u32[]{:S(2)}) collective-permute-start(s16[24,4224]{1,0:T(8,128)(2,1)S(1)} %get-tuple-element.45.refs_3_.refs_1_), channel_id=1, source_target_pairs={{0,4},{4,0},{1,5},{5,1},{2,6},{6,2},{3,7},{7,3},{8,12},{12,8},{9,1... | collective-permute-start | bytes 608264 | tf_op jit(solution)/shard_map/ppermute | solution.py:296
  15.4 10.0 %collective-permute-start.7 = (bf16[24,2048]{1,0:T(8,128)(2,1)S(1)}, bf16[24,2048]{1,0:T(8,128)(2,1)S(1)}, u32[]{:S(2)}, u32[]{:S(2)}) collective-permute-start(bf16[24,2048]{1,0:T(8,128)(2,1)S(1)} %get-tuple-element.48.early_rounded), channel_id=1, source_target_pairs={{0,2},{1,3},{2,0},{3,1},{4,6},{5,7},{6,4},{7,5},{8,10},{9,11},{10,... | collective-permute-start | bytes 294920 | tf_op jit(solution)/shard_map/ppermute | solution.py:296
  18.7 8.4 %collective-permute-start.12 = (bf16[24,2048]{1,0:T(8,128)(2,1)S(1)}, bf16[24,2048]{1,0:T(8,128)(2,1)S(1)}, u32[]{:S(2)}, u32[]{:S(2)}) collective-permute-start(bf16[24,2048]{1,0:T(8,128)(2,1)S(1)} %get-tuple-element.55), channel_id=1, source_target_pairs={{0,2},{1,3},{2,0},{3,1},{4,6},{5,7},{6,4},{7,5},{8,10},{9,11},{10,... | collective-permute-start | bytes 294920 | tf_op jit(solution)/shard_map/ppermute | solution.py:296
  21.0 9.0 %collective-permute-start.6 = (bf16[24,4096]{1,0:T(8,128)(2,1)S(1)}, bf16[24,4096]{1,0:T(8,128)(2,1)S(1)}, u32[]{:S(2)}, u32[]{:S(2)}) collective-permute-start(bf16[24,4096]{1,0:T(8,128)(2,1)S(1)} %get-tuple-element.50.refs_4_.refs_2_), channel_id=1, source_target_pairs={{0,1},{1,0},{2,3},{3,2},{4,5},{5,4},{6,7},{7,6},{8,9},{9,8},{10,11... | collective-permute-start | bytes 589832 | tf_op jit(solution)/shard_map/ppermute | solution.py:296
  23.2 5.8 %collective-permute-start.13 = (s16[24,4224]{1,0:T(8,128)(2,1)S(1)}, s16[24,4224]{1,0:T(8,128)(2,1)S(1)}, u32[]{:S(2)}, u32[]{:S(2)}) collective-permute-start(s16[24,4224]{1,0:T(8,128)(2,1)S(1)} %get-tuple-element.53.refs_3_.refs_1_), channel_id=1, source_target_pairs={{0,4},{4,0},{1,5},{5,1},{2,6},{6,2},{3,7},{7,3},{8,12},{12,8},{9,1... | collective-permute-start | bytes 608264 | tf_op jit(solution)/shard_map/ppermute | solution.py:296
  25.3 7.8 %collective-permute-start.15 = (s16[24,4224]{1,0:T(8,128)(2,1)S(1)}, s16[24,4224]{1,0:T(8,128)(2,1)S(1)}, u32[]{:S(2)}, u32[]{:S(2)}) collective-permute-start(s16[24,4224]{1,0:T(8,128)(2,1)S(1)} %get-tuple-element.54.refs_0_.refs_2_), channel_id=1, source_target_pairs={{0,24},{8,16},{16,8},{24,0},{1,25},{9,17},{17,9},{25,1},{2,26},{10... | collective-permute-start | bytes 608264 | tf_op jit(solution)/shard_map/ppermute | solution.py:296
  25.4 5.6 %collective-permute-start.11 = (bf16[24,2048]{1,0:T(8,128)(2,1)S(1)}, bf16[24,2048]{1,0:T(8,128)(2,1)S(1)}, u32[]{:S(2)}, u32[]{:S(2)}) collective-permute-start(bf16[24,2048]{1,0:T(8,128)(2,1)S(1)} %shard_map.104.refs_0_.refs_4_), channel_id=1, source_target_pairs={{0,1},{1,0},{2,3},{3,2},{4,5},{5,4},{6,7},{7,6},{8,9},{9,8},{10,11... | collective-permute-start | bytes 294920 | tf_op jit(solution)/shard_map/ppermute | solution.py:296
  27.2 5.9 %collective-permute-start.16 = (bf16[24,2048]{1,0:T(8,128)(2,1)S(1)}, bf16[24,2048]{1,0:T(8,128)(2,1)S(1)}, u32[]{:S(2)}, u32[]{:S(2)}) collective-permute-start(bf16[24,2048]{1,0:T(8,128)(2,1)S(1)} %shard_map.106.refs_3_.refs_6_.refs_1_), channel_id=1, source_target_pairs={{0,1},{1,0},{2,3},{3,2},{4,5},{5,4},{6,7},{7,6},{8,9},{9,8},{10,11... | collective-permute-start | bytes 294920 | tf_op jit(solution)/shard_map/ppermute | solution.py:296
  29.0 4.1 %collective-permute-start.14 = (s16[24,4224]{1,0:T(8,128)(2,1)S(1)}, s16[24,4224]{1,0:T(8,128)(2,1)S(1)}, u32[]{:S(2)}, u32[]{:S(2)}) collective-permute-start(s16[24,4224]{1,0:T(8,128)(2,1)S(1)} %shard_map.109), channel_id=1, source_target_pairs={{0,8},{8,0},{16,24},{24,16},{1,9},{9,1},{17,25},{25,17},{2,10},{10... | collective-permute-start | bytes 608264 | tf_op jit(solution)/shard_map/ppermute | solution.py:296

commit v2 on v1

--- a/solution.py
+++ b/solution.py
@@ -8,10 +8,11 @@
 from jax.sharding import PartitionSpec as P
 
 LANES = 128
-STEP = 4 * LANES
+STEP = 8 * LANES
+PARTS = 4
 SCALE = 32767.0
 DIGIT = 1024
-COST = dict(c=4_000_000_000, a2=4_000_000_000, b2=4_000_000_000, d=4_000_000_000, a3=0, b3=4_000_000_000, v=0, m=0, ga=0, gb=10000000000, m4=4_000_000_000, pe=2_000_000_000, v4=0, pl=4_000_000_000, t1=2_000_000_000, t2=2_000_000_000, t3=4_000_000_000, gn=0)
+COST = dict(c=4_000_000_000, a2=4_000_000_000, b2=4_000_000_000, d=4_000_000_000, a3=0, b3=4_000_000_000, v=0, m=0, ga=0, gb=10000000000, m4=4_000_000_000, pe=2000000000, v4=0, pl=4_000_000_000, t1=2000000000, t2=2_000_000_000, t3=4_000_000_000, gn=0, t0=40_000_000_000, gz=2000000000)
 
 
 def coded(x):
@@ -67,18 +68,9 @@
     return 0.95 * moment_two + 0.05 * grad * grad
 
 
-def early_kernel(master, moment_one, moment_two, grads, counts, step, state, sent, weight_out, fixes, *refs):
-    ins, (counts_in, sems) = refs[:4], refs[4:]
-    part = state.shape[1]
-    low = pl.ds(0, part)
-    pairs = [(counts, counts_in)]
-    pairs += [(a.at[:, low], b) for a, b in zip((moment_two, grads, moment_one, master), ins)]
-    copies = [pltpu.make_async_copy(a, b, sems.at[i]) for i, (a, b) in enumerate(pairs)]
-    for copy in copies:
-        copy.start()
-    copies[0].wait()
+def early_kernel(master, moment_one, moment_two, grads, counts, step, state, sent, weight_out, fixes):
     shape = (master.shape[0], LANES)
-    many = counts_in[...]
+    many = counts[...]
     lengths = lax.shift_left(jnp.ones_like(many), lax.broadcasted_iota(jnp.int32, many.shape, 1))
     total = jnp.sum((many * lengths).astype(jnp.float32), axis=1, keepdims=True)
     weight = jnp.broadcast_to(total, shape)
@@ -89,20 +81,17 @@
     fix_second = 1.0 / (1.0 - jnp.exp(steps * math.log(0.95)))
     fixes[0] = fix_first
     fixes[1] = fix_second
-    for copy in copies[1:]:
-        copy.wait()
-    second_in, grads_in, first_in, master_in = ins
 
     def body(start):
         at = lanes(start)
-        grad = grads_in[:, at].astype(jnp.float32)
-        first = first_of(first_in[:, at], grad)
-        second = second_of(second_in[:, at], grad)
-        new = stepped(master_in[:, at], first, second, fix_first, fix_second)
+        grad = grads[:, at].astype(jnp.float32)
+        first = first_of(moment_one[:, at], grad)
+        second = second_of(moment_two[:, at], grad)
+        new = stepped(master[:, at], first, second, fix_first, fix_second)
         state[:, at] = new
         sent[:, at] = coded(new)
 
-    over_lanes(part, body)
+    over_lanes(state.shape[1], body)
 
 
 def late_kernel(master, moment_one, moment_two, grads, weight, fixes, state, sent):
@@ -208,9 +197,9 @@
 
 def last_moment(state, own, others, factors, new, result, sems):
     _, at_lanes = merged(state, own, others, factors)
-    part = new.shape[1] // 2
+    part = new.shape[1] // PARTS
     copies = []
-    for i in range(2):
+    for i in range(PARTS):
 
         def body(start, base=i * part):
             at = lanes(start, base)
@@ -347,16 +336,9 @@
     early, sent_early, weight, fixes = local(
         early_kernel,
         [(low_part, f32), with_weight(low_part), (tile, f32), ((2, *tile), f32)],
-        [*[pltpu.with_memory_space_constraint(a, pltpu.HBM) for a in (*own, counts.reshape(1, -1))], step],
-        [HBM] * 5 + [SMEM],
-        scratch=[
-            pltpu.VMEM(low_part, f32),
-            pltpu.VMEM(low_part, bf16),
-            pltpu.VMEM(low_part, f32),
-            pltpu.VMEM(low_part, f32),
-            pltpu.VMEM((1, counts.shape[2]), jnp.int32),
-            pltpu.SemaphoreType.DMA((5,)),
-        ],
+        [*own, counts.reshape(1, -1), step],
+        [VMEM] * 5 + [SMEM],
+        after=turn([], COST["t0"]),
     )
     late, sent_late = local(
         late_kernel, [(high_part, f32), with_weight(high_part)], [*own, weight, fixes], after=[sent_early]
@@ -393,7 +375,7 @@
         (late, sent_late, rounded_early, *others),
         cost=COST["b3"],
     )
-    halves = [{0: rounded_early}, {0: rounded_late}]
+    halves = [{0: rounded_early}, {0: held_until(rounded_late, [rounded], COST["gz"])}]
     far = n // 2
     while far > 1:
         halves = [exchanged(held, "fsdp", far) for held in halves]
@@ -414,7 +396,7 @@
         [(full, f32), DONE],
         (first, sent_first, *others),
         out_specs=[HBM, VMEM],
-        scratch=[pltpu.VMEM(full, f32), pltpu.SemaphoreType.DMA((2,))],
+        scratch=[pltpu.VMEM(full, f32), pltpu.SemaphoreType.DMA((PARTS,))],
         after=[halves[1][2]],
         cost=COST["m4"],
     )
@@ -439,7 +421,7 @@
         (whole, second, sent_second, *others, *blocks),
         [HBM] + [VMEM] * (2 + len(others) + len(blocks)),
         [HBM, HBM],
-        scratch=[pltpu.VMEM(full, f32), pltpu.SemaphoreType.DMA((2,)), pltpu.SemaphoreType.DMA((len(blocks),))],
+        scratch=[pltpu.VMEM(full, f32), pltpu.SemaphoreType.DMA((PARTS,)), pltpu.SemaphoreType.DMA((len(blocks),))],
         after=turn([done, *blocks], COST["t3"]),
         cost=COST["v4"],
         aliases={0: 0},

time: 34.3 us -> 33.7 us (0.983)
  Pallas kernels: 8.1 us -> 6.06 us
  starting transfers between devices: 19.9 us -> 21.4 us
  waiting for transfers between devices: 4.67 us -> 3.72 us
  local copies, waits for them, and re-layouts: 0.02 us -> 0.77 us
    pallas_call x19 -> x21, Pallas kernels: 8.1 us -> 6.06 us  [local(): pl.pallas_call(ordered_kernel if after else kernel, out_shape=[jax.ShapeD...]
    ppermute x17, starting transfers between devices: 19.9 us -> 21.4 us  [along(): lax.ppermute(block, axis, [(i, partner(i)) for i in range(lax.axis_size(a...]
    ppermute x17, waiting for transfers between devices: 4.67 us -> 3.72 us  [along(): lax.ppermute(block, axis, [(i, partner(i)) for i in range(lax.axis_size(a...]
    unnamed x8 -> x10, local copies, waits for them, and re-layouts: 0.02 us -> 0.77 us
  transfers between devices with their start and end apart: 17 -> 17, of which waited for: 6 -> 5; matrix products, arithmetic and copies ran while one was open for 0% -> 0% of each run, Pallas kernels for 16% -> 14%
where the time goes in v2:
time: 33.7 us; the launch traced here: 33.5 us
  starting transfers between devices  21.4 us (64%)
  Pallas kernels  6.06 us (18%)
  waiting for transfers between devices  3.72 us (11%)
  between operations  1.58 us (5%)
  local copies, waits for them, and re-layouts  0.77 us (2%)
    ppermute x17, starting transfers between devices, along(): lax.ppermute(block, axis, [(i, partner(i)) for i in range(lax.axis_size(a...  21.4 us
    pallas_call x21, Pallas kernels, local(): pl.pallas_call(ordered_kernel if after else kernel, out_shape=[jax.ShapeD...  6.06 us
    ppermute x17, waiting for transfers between devices, along(): lax.ppermute(block, axis, [(i, partner(i)) for i in range(lax.axis_size(a...  3.72 us
    unnamed x10, local copies, waits for them, and re-layouts  0.77 us
  transfers between devices with their start and end apart: 17, of which 5 were waited for; matrix products, arithmetic and copies ran while one was open for 0% of the time, Pallas kernels for 14%

profile of v2, /device:TPU:0, one launch (start us, length us, event | category | flops | bytes accessed | tf_op | source)
XLA Modules:
  0.0 33.5 jit_solution(7098414803903013955)
XLA Ops:
  1.4 0.0 copy-start.4
  1.4 0.1 copy-done.3
  1.6 0.2 copy-done.2
  1.8 0.1 copy-done.1
  1.9 0.1 copy-done
  2.0 0.2 copy-done.4
  2.2 0.3 %shard_map.94 = (f32[24,2048]{1,0:T(8,128)S(1)}, s16[24,2176]{1,0:T(8,128)(2,1)S(1)}, f32[24,128]{1,0:T(8,128)S(1)}, f32[2,24,128]{2,1,0:T(8,128)S(1)}) custom-call(f32[24,4096]{1,0:T(8,128)S(1)} %bitcast.9, f32[24,4096]{1,0:T(8,128)S(1)} %bitcast.11, f32[24,4096]{1,0:T(8,128)S(1)} %bitcast.14, bf16[24,4096]{1,0:T(8,128)(2,1)S(1)} %bitcast.17, ...), custom_call_target="tpu_custom_call" | custom-call | tf_op jit(solution)/shard_map/pallas_call | solution.py:272
  2.6 2.5 %collective-permute-start.1 = (s16[24,2176]{1,0:T(8,128)(2,1)S(1)}, s16[24,2176]{1,0:T(8,128)(2,1)S(1)}, u32[]{:S(2)}, u32[]{:S(2)}) collective-permute-start(s16[24,2176]{1,0:T(8,128)(2,1)S(1)} %get-tuple-element.36.refs_6_.refs_1_), channel_id=1, source_target_pairs={{0,24},{8,16},{16,8},{24,0},{1,25},{9,17},{17,9},{25,1},{2,26},{10... | collective-permute-start | bytes 313352 | tf_op jit(solution)/shard_map/ppermute | solution.py:285
  5.0 0.7 %collective-permute-start = (s16[24,2176]{1,0:T(8,128)(2,1)S(1)}, s16[24,2176]{1,0:T(8,128)(2,1)S(1)}, u32[]{:S(2)}, u32[]{:S(2)}) collective-permute-start(s16[24,2176]{1,0:T(8,128)(2,1)S(1)} %get-tuple-element.36.refs_6_.refs_1_), channel_id=1, source_target_pairs={{0,8},{8,0},{16,24},{24,16},{1,9},{9,1},{17,25},{25,17},{2,10},{10... | collective-permute-start | bytes 313352 | tf_op jit(solution)/shard_map/ppermute | solution.py:285
  5.7 0.3 shard_map.95
  6.0 0.1 collective-permute-start.4
  6.1 0.0 collective-permute-start.3
  6.1 0.3 shard_map.96
  6.4 1.7 %collective-permute-start.10 = (s16[24,4224]{1,0:T(8,128)(2,1)S(1)}, s16[24,4224]{1,0:T(8,128)(2,1)S(1)}, u32[]{:S(2)}, u32[]{:S(2)}) collective-permute-start(s16[24,4224]{1,0:T(8,128)(2,1)S(1)} %get-tuple-element.40.refs_4_.refs_1_), channel_id=1, source_target_pairs={{0,24},{8,16},{16,8},{24,0},{1,25},{9,17},{17,9},{25,1},{2,26},{10... | collective-permute-start | bytes 608264 | tf_op jit(solution)/shard_map/ppermute | solution.py:285
  8.1 0.2 collective-permute-done.1.refs_3_
  8.3 0.3 collective-permute-start.9
  8.6 0.0 collective-permute-done.refs_2_
  8.6 0.3 shard_map.97
  9.0 2.4 %collective-permute-start.2 = (s16[24,2176]{1,0:T(8,128)(2,1)S(1)}, s16[24,2176]{1,0:T(8,128)(2,1)S(1)}, u32[]{:S(2)}, u32[]{:S(2)}) collective-permute-start(s16[24,2176]{1,0:T(8,128)(2,1)S(1)} %get-tuple-element.42.refs_4_.refs_1_), channel_id=1, source_target_pairs={{0,4},{4,0},{1,5},{5,1},{2,6},{6,2},{3,7},{7,3},{8,12},{12,8},{9,1... | collective-permute-start | bytes 313352 | tf_op jit(solution)/shard_map/ppermute | solution.py:285
  11.4 0.0 collective-permute-done.4.refs_3_
  11.4 0.0 collective-permute-done.3.refs_2_
  11.4 0.3 shard_map.98
  11.7 1.6 %collective-permute-start.5 = (s16[24,2176]{1,0:T(8,128)(2,1)S(1)}, s16[24,2176]{1,0:T(8,128)(2,1)S(1)}, u32[]{:S(2)}, u32[]{:S(2)}) collective-permute-start(s16[24,2176]{1,0:T(8,128)(2,1)S(1)} %get-tuple-element.44.refs_3_.own), channel_id=1, source_target_pairs={{0,4},{4,0},{1,5},{5,1},{2,6},{6,2},{3,7},{7,3},{8,12},{12,8},{9,1... | collective-permute-start | bytes 313352 | tf_op jit(solution)/shard_map/ppermute | solution.py:285
  13.3 0.3 shard_map.99
  13.6 0.5 %collective-permute-start.8 = (s16[24,4224]{1,0:T(8,128)(2,1)S(1)}, s16[24,4224]{1,0:T(8,128)(2,1)S(1)}, u32[]{:S(2)}, u32[]{:S(2)}) collective-permute-start(s16[24,4224]{1,0:T(8,128)(2,1)S(1)} %get-tuple-element.45.refs_3_.refs_1_), channel_id=1, source_target_pairs={{0,4},{4,0},{1,5},{5,1},{2,6},{6,2},{3,7},{7,3},{8,12},{12,8},{9,1... | collective-permute-start | bytes 608264 | tf_op jit(solution)/shard_map/ppermute | solution.py:285
  14.1 0.7 %collective-permute-done.2.refs_2_ = s16[24,2176]{1,0:T(8,128)(2,1)S(1)} collective-permute-done((s16[24,2176]{1,0:T(8,128)(2,1)S(1)}, s16[24,2176]{1,0:T(8,128)(2,1)S(1)}, u32[]{:S(2)}, u32[]{:S(2)}) %collective-permute-start.2) | collective-permute-done | bytes 104480 | tf_op jit(solution)/shard_map/ppermute | solution.py:285
  14.8 0.2 shard_map.100
  15.0 3.0 %collective-permute-start.7 = (bf16[24,2048]{1,0:T(8,128)(2,1)S(1)}, bf16[24,2048]{1,0:T(8,128)(2,1)S(1)}, u32[]{:S(2)}, u32[]{:S(2)}) collective-permute-start(bf16[24,2048]{1,0:T(8,128)(2,1)S(1)} %get-tuple-element.48.early_rounded), channel_id=1, source_target_pairs={{0,2},{1,3},{2,0},{3,1},{4,6},{5,7},{6,4},{7,5},{8,10},{9,11},{10,... | collective-permute-start | bytes 294920 | tf_op jit(solution)/shard_map/ppermute | solution.py:285
  18.0 0.0 collective-permute-done.5.refs_0_
  18.0 0.2 shard_map.101
  18.2 1.6 %collective-permute-start.6 = (bf16[24,4096]{1,0:T(8,128)(2,1)S(1)}, bf16[24,4096]{1,0:T(8,128)(2,1)S(1)}, u32[]{:S(2)}, u32[]{:S(2)}) collective-permute-start(bf16[24,4096]{1,0:T(8,128)(2,1)S(1)} %get-tuple-element.50.refs_4_.refs_1_.refs_2_), channel_id=1, source_target_pairs={{0,1},{1,0},{2,3},{3,2},{4,5},{5,4},{6,7},{7,6},{8,9},{9,8},{10,11... | collective-permute-start | bytes 589832 | tf_op jit(solution)/shard_map/ppermute | solution.py:285
  19.9 0.0 collective-permute-done.10.refs_3_
  19.9 2.2 %collective-permute-start.12 = (bf16[24,2048]{1,0:T(8,128)(2,1)S(1)}, bf16[24,2048]{1,0:T(8,128)(2,1)S(1)}, u32[]{:S(2)}, u32[]{:S(2)}) collective-permute-start(bf16[24,2048]{1,0:T(8,128)(2,1)S(1)} %shard_map.106), channel_id=1, source_target_pairs={{0,2},{1,3},{2,0},{3,1},{4,6},{5,7},{6,4},{7,5},{8,10},{9,11},{10,... | collective-permute-start | bytes 294920 | tf_op jit(solution)/shard_map/ppermute | solution.py:285
  22.1 0.0 collective-permute-done.9.refs_2_
  22.1 0.6 %shard_map.102 = (f32[24,4096]{1,0:T(8,128)S(1)}, s16[24,4224]{1,0:T(8,128)(2,1)S(1)}) custom-call(f32[24,4096]{1,0:T(8,128)S(1)} %get-tuple-element.52.refs_0_, s16[24,4224]{1,0:T(8,128)(2,1)S(1)} %get-tuple-element.40.refs_4_.refs_1_, s16[24,4224]{1,0:T(8,128)(2,1)S(1)} %collective-permute-done.9.refs_2_, ...), custom_call_target="tpu_custom_call" | custom-call | tf_op jit(solution)/shard_map/pallas_call | solution.py:272
  22.6 1.6 %collective-permute-start.13 = (s16[24,4224]{1,0:T(8,128)(2,1)S(1)}, s16[24,4224]{1,0:T(8,128)(2,1)S(1)}, u32[]{:S(2)}, u32[]{:S(2)}) collective-permute-start(s16[24,4224]{1,0:T(8,128)(2,1)S(1)} %get-tuple-element.53.refs_3_.refs_1_), channel_id=1, source_target_pairs={{0,4},{4,0},{1,5},{5,1},{2,6},{6,2},{3,7},{7,3},{8,12},{12,8},{9,1... | collective-permute-start | bytes 608264 | tf_op jit(solution)/shard_map/ppermute | solution.py:285
  24.2 0.0 collective-permute-done.8.refs_2_
  24.2 0.4 %shard_map.103 = (f32[24,4096]{1,0:T(8,128)S(1)}, s16[24,4224]{1,0:T(8,128)(2,1)S(1)}, s16[24,4224]{1,0:T(8,128)(2,1)S(1)}) custom-call(f32[24,4096]{1,0:T(8,128)S(1)} %get-tuple-element.51.refs_0_, s16[24,4224]{1,0:T(8,128)(2,1)S(1)} %get-tuple-element.45.refs_3_.refs_1_, s16[24,4224]{1,0:T(8,128)(2,1)S(1)} %collective-permute-done.8.refs_2_, ...), custom_call_target="tpu_custom_call" | custom-call | tf_op jit(solution)/shard_map/pallas_call | solution.py:272
  24.6 0.1 collective-permute-start.15
  24.7 0.5 %collective-permute-start.11 = (bf16[24,2048]{1,0:T(8,128)(2,1)S(1)}, bf16[24,2048]{1,0:T(8,128)(2,1)S(1)}, u32[]{:S(2)}, u32[]{:S(2)}) collective-permute-start(bf16[24,2048]{1,0:T(8,128)(2,1)S(1)} %shard_map.105.refs_0_.refs_4_), channel_id=1, source_target_pairs={{0,1},{1,0},{2,3},{3,2},{4,5},{5,4},{6,7},{7,6},{8,9},{9,8},{10,11... | collective-permute-start | bytes 294920 | tf_op jit(solution)/shard_map/ppermute | solution.py:285
  25.2 1.1 %collective-permute-done.12.refs_0_ = bf16[24,2048]{1,0:T(8,128)(2,1)S(1)} collective-permute-done((bf16[24,2048]{1,0:T(8,128)(2,1)S(1)}, bf16[24,2048]{1,0:T(8,128)(2,1)S(1)}, u32[]{:S(2)}, u32[]{:S(2)}) %collective-permute-start.12) | collective-permute-done | bytes 98336 | tf_op jit(solution)/shard_map/ppermute | solution.py:285
  26.3 2.5 %collective-permute-start.16 = (bf16[24,2048]{1,0:T(8,128)(2,1)S(1)}, bf16[24,2048]{1,0:T(8,128)(2,1)S(1)}, u32[]{:S(2)}, u32[]{:S(2)}) collective-permute-start(bf16[24,2048]{1,0:T(8,128)(2,1)S(1)} %shard_map.108.refs_3_.refs_6_.refs_1_), channel_id=1, source_target_pairs={{0,1},{1,0},{2,3},{3,2},{4,5},{5,4},{6,7},{7,6},{8,9},{9,8},{10,11... | collective-permute-start | bytes 294920 | tf_op jit(solution)/shard_map/ppermute | solution.py:285
  28.8 0.9 %shard_map.109 = (f32[24,4096]{1,0:T(8,128)}, f32[8,128]{1,0:T(8,128)S(1)}) custom-call(f32[24,4096]{1,0:T(8,128)S(1)} %get-tuple-element.56.refs_0_, s16[24,4224]{1,0:T(8,128)(2,1)S(1)} %get-tuple-element.53.refs_3_.refs_1_, s16[24,4224]{1,0:T(8,128)(2,1)S(1)} %collective-permute-done.13.refs_2_, bf16[24,2048]{1,0:T(8,128)(2,1)S(1)} %shard_map.108.refs_3_.refs_6_.refs_1_), custom_call_target="tpu_custom_call" | custom-call | flops 4000000000 | tf_op jit(solution)/shard_map/pallas_call | solution.py:272
  29.7 0.1 collective-permute-done.11.refs_5_
  29.9 1.0 %shard_map.110 = (bf16[4,24,4096]{2,1,0:T(8,128)(2,1)}, f32[24,4096]{1,0:T(8,128)}, f32[8,128]{1,0:T(8,128)S(1)}) custom-call(f32[24,2048]{1,0:T(8,128)S(1)} %get-tuple-element.46.refs_0_, f32[24,2048]{1,0:T(8,128)S(1)} %get-tuple-element.49.refs_1_, bf16[24,4096]{1,0:T(8,128)(2,1)S(1)} %get-tuple-element.50.refs_4_.refs_1_.refs_2_, ...), custom_call_target="tpu_custom_call" | custom-call | flops 2000000000 | tf_op jit(solution)/shard_map/pallas_call | solution.py:272
  30.9 1.6 %collective-permute-done.16.refs_1_.refs_5_ = bf16[24,2048]{1,0:T(8,128)(2,1)S(1)} collective-permute-done((bf16[24,2048]{1,0:T(8,128)(2,1)S(1)}, bf16[24,2048]{1,0:T(8,128)(2,1)S(1)}, u32[]{:S(2)}, u32[]{:S(2)}) %collective-permute-start.16) | collective-permute-done | bytes 98336 | tf_op jit(solution)/shard_map/ppermute | solution.py:285
  32.5 0.0 collective-permute-done.14.refs_3_
  32.5 1.0 %shard_map.113 = (bf16[4,24,4096]{2,1,0:T(8,128)(2,1)}, f32[24,4096]{1,0:T(8,128)}) custom-call(bf16[4,24,4096]{2,1,0:T(8,128)(2,1)} %get-tuple-element.60.refs_0_, f32[24,4096]{1,0:T(8,128)S(1)} %get-tuple-element.61.refs_1_, s16[24,4224]{1,0:T(8,128)(2,1)S(1)} %get-tuple-element.54.refs_0_.refs_2_, ...), custom_call_target="tpu_custom_call", output_to_operand_aliasing={{0}: (0, {})} | custom-call | tf_op jit(solution)/shard_map/pallas_call | solution.py:272
  (17 shorter events, 0.0 us)
Async XLA Ops:
  0.6 0.9 %copy-start.3 = (bf16[1,1,24,4096]{3,2,1,0:T(8,128)(2,1)S(1)}, bf16[1,1,24,4096]{3,2,1,0:T(8,128)(2,1)}, u32[]{:S(2)}) copy-start(bf16[1,1,24,4096]{3,2,1,0:T(8,128)(2,1)} %param.9) | copy-start | bytes 589828
  0.6 1.1 %copy-start.2 = (f32[1,1,24,4096]{3,2,1,0:T(8,128)S(1)}, f32[1,1,24,4096]{3,2,1,0:T(8,128)}, u32[]{:S(2)}) copy-start(f32[1,1,24,4096]{3,2,1,0:T(8,128)} %param.8) | copy-start | bytes 1179652
  0.7 1.2 %copy-start.1 = (f32[1,1,24,4096]{3,2,1,0:T(8,128)S(1)}, f32[1,1,24,4096]{3,2,1,0:T(8,128)}, u32[]{:S(2)}) copy-start(f32[1,1,24,4096]{3,2,1,0:T(8,128)} %param.7) | copy-start | bytes 1179652
  0.7 1.3 %copy-start = (f32[1,1,24,4096]{3,2,1,0:T(8,128)S(1)}, f32[1,1,24,4096]{3,2,1,0:T(8,128)}, u32[]{:S(2)}) copy-start(f32[1,1,24,4096]{3,2,1,0:T(8,128)} %param.6) | copy-start | bytes 1179652
  1.4 0.8 %copy-start.4 = (s32[1,1,8]{2,1,0:T(1,128)S(1)}, s32[1,1,8]{2,1,0:T(1,128)}, u32[]{:S(2)}) copy-start(s32[1,1,8]{2,1,0:T(1,128)} %param.10) | copy-start | bytes 100
  2.6 5.8 %collective-permute-start.1 = (s16[24,2176]{1,0:T(8,128)(2,1)S(1)}, s16[24,2176]{1,0:T(8,128)(2,1)S(1)}, u32[]{:S(2)}, u32[]{:S(2)}) collective-permute-start(s16[24,2176]{1,0:T(8,128)(2,1)S(1)} %get-tuple-element.36.refs_6_.refs_1_), channel_id=1, source_target_pairs={{0,24},{8,16},{16,8},{24,0},{1,25},{9,17},{17,9},{25,1},{2,26},{10... | collective-permute-start | bytes 313352 | tf_op jit(solution)/shard_map/ppermute | solution.py:285
  5.0 3.6 %collective-permute-start = (s16[24,2176]{1,0:T(8,128)(2,1)S(1)}, s16[24,2176]{1,0:T(8,128)(2,1)S(1)}, u32[]{:S(2)}, u32[]{:S(2)}) collective-permute-start(s16[24,2176]{1,0:T(8,128)(2,1)S(1)} %get-tuple-element.36.refs_6_.refs_1_), channel_id=1, source_target_pairs={{0,8},{8,0},{16,24},{24,16},{1,9},{9,1},{17,25},{25,17},{2,10},{10... | collective-permute-start | bytes 313352 | tf_op jit(solution)/shard_map/ppermute | solution.py:285
  6.0 5.4 %collective-permute-start.4 = (s16[24,2176]{1,0:T(8,128)(2,1)S(1)}, s16[24,2176]{1,0:T(8,128)(2,1)S(1)}, u32[]{:S(2)}, u32[]{:S(2)}) collective-permute-start(s16[24,2176]{1,0:T(8,128)(2,1)S(1)} %get-tuple-element.39.refs_3_.refs_1_), channel_id=1, source_target_pairs={{0,24},{8,16},{16,8},{24,0},{1,25},{9,17},{17,9},{25,1},{2,26},{10... | collective-permute-start | bytes 313352 | tf_op jit(solution)/shard_map/ppermute | solution.py:285
  6.1 5.3 %collective-permute-start.3 = (s16[24,2176]{1,0:T(8,128)(2,1)S(1)}, s16[24,2176]{1,0:T(8,128)(2,1)S(1)}, u32[]{:S(2)}, u32[]{:S(2)}) collective-permute-start(s16[24,2176]{1,0:T(8,128)(2,1)S(1)} %get-tuple-element.39.refs_3_.refs_1_), channel_id=1, source_target_pairs={{0,8},{8,0},{16,24},{24,16},{1,9},{9,1},{17,25},{25,17},{2,10},{10... | collective-permute-start | bytes 313352 | tf_op jit(solution)/shard_map/ppermute | solution.py:285
  6.4 13.5 %collective-permute-start.10 = (s16[24,4224]{1,0:T(8,128)(2,1)S(1)}, s16[24,4224]{1,0:T(8,128)(2,1)S(1)}, u32[]{:S(2)}, u32[]{:S(2)}) collective-permute-start(s16[24,4224]{1,0:T(8,128)(2,1)S(1)} %get-tuple-element.40.refs_4_.refs_1_), channel_id=1, source_target_pairs={{0,24},{8,16},{16,8},{24,0},{1,25},{9,17},{17,9},{25,1},{2,26},{10... | collective-permute-start | bytes 608264 | tf_op jit(solution)/shard_map/ppermute | solution.py:285
  8.3 13.7 %collective-permute-start.9 = (s16[24,4224]{1,0:T(8,128)(2,1)S(1)}, s16[24,4224]{1,0:T(8,128)(2,1)S(1)}, u32[]{:S(2)}, u32[]{:S(2)}) collective-permute-start(s16[24,4224]{1,0:T(8,128)(2,1)S(1)} %get-tuple-element.40.refs_4_.refs_1_), channel_id=1, source_target_pairs={{0,8},{8,0},{16,24},{24,16},{1,9},{9,1},{17,25},{25,17},{2,10},{10... | collective-permute-start | bytes 608264 | tf_op jit(solution)/shard_map/ppermute | solution.py:285
  9.0 5.8 %collective-permute-start.2 = (s16[24,2176]{1,0:T(8,128)(2,1)S(1)}, s16[24,2176]{1,0:T(8,128)(2,1)S(1)}, u32[]{:S(2)}, u32[]{:S(2)}) collective-permute-start(s16[24,2176]{1,0:T(8,128)(2,1)S(1)} %get-tuple-element.42.refs_4_.refs_1_), channel_id=1, source_target_pairs={{0,4},{4,0},{1,5},{5,1},{2,6},{6,2},{3,7},{7,3},{8,12},{12,8},{9,1... | collective-permute-start | bytes 313352 | tf_op jit(solution)/shard_map/ppermute | solution.py:285
  11.7 6.3 %collective-permute-start.5 = (s16[24,2176]{1,0:T(8,128)(2,1)S(1)}, s16[24,2176]{1,0:T(8,128)(2,1)S(1)}, u32[]{:S(2)}, u32[]{:S(2)}) collective-permute-start(s16[24,2176]{1,0:T(8,128)(2,1)S(1)} %get-tuple-element.44.refs_3_.own), channel_id=1, source_target_pairs={{0,4},{4,0},{1,5},{5,1},{2,6},{6,2},{3,7},{7,3},{8,12},{12,8},{9,1... | collective-permute-start | bytes 313352 | tf_op jit(solution)/shard_map/ppermute | solution.py:285
  13.6 10.6 %collective-permute-start.8 = (s16[24,4224]{1,0:T(8,128)(2,1)S(1)}, s16[24,4224]{1,0:T(8,128)(2,1)S(1)}, u32[]{:S(2)}, u32[]{:S(2)}) collective-permute-start(s16[24,4224]{1,0:T(8,128)(2,1)S(1)} %get-tuple-element.45.refs_3_.refs_1_), channel_id=1, source_target_pairs={{0,4},{4,0},{1,5},{5,1},{2,6},{6,2},{3,7},{7,3},{8,12},{12,8},{9,1... | collective-permute-start | bytes 608264 | tf_op jit(solution)/shard_map/ppermute | solution.py:285
  15.0 9.7 %collective-permute-start.7 = (bf16[24,2048]{1,0:T(8,128)(2,1)S(1)}, bf16[24,2048]{1,0:T(8,128)(2,1)S(1)}, u32[]{:S(2)}, u32[]{:S(2)}) collective-permute-start(bf16[24,2048]{1,0:T(8,128)(2,1)S(1)} %get-tuple-element.48.early_rounded), channel_id=1, source_target_pairs={{0,2},{1,3},{2,0},{3,1},{4,6},{5,7},{6,4},{7,5},{8,10},{9,11},{10,... | collective-permute-start | bytes 294920 | tf_op jit(solution)/shard_map/ppermute | solution.py:285
  18.2 11.5 %collective-permute-start.6 = (bf16[24,4096]{1,0:T(8,128)(2,1)S(1)}, bf16[24,4096]{1,0:T(8,128)(2,1)S(1)}, u32[]{:S(2)}, u32[]{:S(2)}) collective-permute-start(bf16[24,4096]{1,0:T(8,128)(2,1)S(1)} %get-tuple-element.50.refs_4_.refs_1_.refs_2_), channel_id=1, source_target_pairs={{0,1},{1,0},{2,3},{3,2},{4,5},{5,4},{6,7},{7,6},{8,9},{9,8},{10,11... | collective-permute-start | bytes 589832 | tf_op jit(solution)/shard_map/ppermute | solution.py:285
  19.9 6.4 %collective-permute-start.12 = (bf16[24,2048]{1,0:T(8,128)(2,1)S(1)}, bf16[24,2048]{1,0:T(8,128)(2,1)S(1)}, u32[]{:S(2)}, u32[]{:S(2)}) collective-permute-start(bf16[24,2048]{1,0:T(8,128)(2,1)S(1)} %shard_map.106), channel_id=1, source_target_pairs={{0,2},{1,3},{2,0},{3,1},{4,6},{5,7},{6,4},{7,5},{8,10},{9,11},{10,... | collective-permute-start | bytes 294920 | tf_op jit(solution)/shard_map/ppermute | solution.py:285
  22.6 6.2 %collective-permute-start.13 = (s16[24,4224]{1,0:T(8,128)(2,1)S(1)}, s16[24,4224]{1,0:T(8,128)(2,1)S(1)}, u32[]{:S(2)}, u32[]{:S(2)}) collective-permute-start(s16[24,4224]{1,0:T(8,128)(2,1)S(1)} %get-tuple-element.53.refs_3_.refs_1_), channel_id=1, source_target_pairs={{0,4},{4,0},{1,5},{5,1},{2,6},{6,2},{3,7},{7,3},{8,12},{12,8},{9,1... | collective-permute-start | bytes 608264 | tf_op jit(solution)/shard_map/ppermute | solution.py:285
  24.6 7.9 %collective-permute-start.15 = (s16[24,4224]{1,0:T(8,128)(2,1)S(1)}, s16[24,4224]{1,0:T(8,128)(2,1)S(1)}, u32[]{:S(2)}, u32[]{:S(2)}) collective-permute-start(s16[24,4224]{1,0:T(8,128)(2,1)S(1)} %get-tuple-element.54.refs_0_.refs_2_), channel_id=1, source_target_pairs={{0,24},{8,16},{16,8},{24,0},{1,25},{9,17},{17,9},{25,1},{2,26},{10... | collective-permute-start | bytes 608264 | tf_op jit(solution)/shard_map/ppermute | solution.py:285
  24.7 5.1 %collective-permute-start.11 = (bf16[24,2048]{1,0:T(8,128)(2,1)S(1)}, bf16[24,2048]{1,0:T(8,128)(2,1)S(1)}, u32[]{:S(2)}, u32[]{:S(2)}) collective-permute-start(bf16[24,2048]{1,0:T(8,128)(2,1)S(1)} %shard_map.105.refs_0_.refs_4_), channel_id=1, source_target_pairs={{0,1},{1,0},{2,3},{3,2},{4,5},{5,4},{6,7},{7,6},{8,9},{9,8},{10,11... | collective-permute-start | bytes 294920 | tf_op jit(solution)/shard_map/ppermute | solution.py:285
  26.3 6.2 %collective-permute-start.16 = (bf16[24,2048]{1,0:T(8,128)(2,1)S(1)}, bf16[24,2048]{1,0:T(8,128)(2,1)S(1)}, u32[]{:S(2)}, u32[]{:S(2)}) collective-permute-start(bf16[24,2048]{1,0:T(8,128)(2,1)S(1)} %shard_map.108.refs_3_.refs_6_.refs_1_), channel_id=1, source_target_pairs={{0,1},{1,0},{2,3},{3,2},{4,5},{5,4},{6,7},{7,6},{8,9},{9,8},{10,11... | collective-permute-start | bytes 294920 | tf_op jit(solution)/shard_map/ppermute | solution.py:285
  28.8 3.7 %collective-permute-start.14 = (s16[24,4224]{1,0:T(8,128)(2,1)S(1)}, s16[24,4224]{1,0:T(8,128)(2,1)S(1)}, u32[]{:S(2)}, u32[]{:S(2)}) collective-permute-start(s16[24,4224]{1,0:T(8,128)(2,1)S(1)} %shard_map.111), channel_id=1, source_target_pairs={{0,8},{8,0},{16,24},{24,16},{1,9},{9,1},{17,25},{25,17},{2,10},{10... | collective-permute-start | bytes 608264 | tf_op jit(solution)/shard_map/ppermute | solution.py:285

commit v3 on v2

--- a/solution.py
+++ b/solution.py
@@ -8,7 +8,7 @@
 from jax.sharding import PartitionSpec as P
 
 LANES = 128
-STEP = 8 * LANES
+STEP = 32 * LANES
 PARTS = 4
 SCALE = 32767.0
 DIGIT = 1024

time: 33.7 us -> 33.3 us (0.988)
  Pallas kernels: 6.06 us -> 5.38 us
    pallas_call x21, Pallas kernels: 6.06 us -> 5.38 us  [local(): pl.pallas_call(ordered_kernel if after else kernel, out_shape=[jax.ShapeD...]
  transfers between devices with their start and end apart: 17 -> 17, of which waited for: 5 -> 4; matrix products, arithmetic and copies ran while one was open for 0% -> 0% of each run, Pallas kernels for 14% -> 12%
where the time goes in v3:
time: 33.3 us; the launch traced here: 33.1 us
  starting transfers between devices  21.5 us (65%)
  Pallas kernels  5.38 us (16%)
  waiting for transfers between devices  3.89 us (12%)
  between operations  1.56 us (5%)
  local copies, waits for them, and re-layouts  0.77 us (2%)
    ppermute x17, starting transfers between devices, along(): lax.ppermute(block, axis, [(i, partner(i)) for i in range(lax.axis_size(a...  21.5 us
    pallas_call x21, Pallas kernels, local(): pl.pallas_call(ordered_kernel if after else kernel, out_shape=[jax.ShapeD...  5.38 us
    ppermute x17, waiting for transfers between devices, along(): lax.ppermute(block, axis, [(i, partner(i)) for i in range(lax.axis_size(a...  3.89 us
    unnamed x10, local copies, waits for them, and re-layouts  0.77 us
  transfers between devices with their start and end apart: 17, of which 4 were waited for; matrix products, arithmetic and copies ran while one was open for 0% of the time, Pallas kernels for 12%

profile of v3, /device:TPU:0, one launch (start us, length us, event | category | flops | bytes accessed | tf_op | source)
XLA Modules:
  0.0 33.1 jit_solution(11940112833676344947)
XLA Ops:
  1.4 0.0 copy-start.4
  1.4 0.1 copy-done.3
  1.6 0.2 copy-done.2
  1.8 0.1 copy-done.1
  1.9 0.1 copy-done
  2.0 0.2 copy-done.4
  2.2 0.2 shard_map.94
  2.5 2.5 %collective-permute-start.1 = (s16[24,2176]{1,0:T(8,128)(2,1)S(1)}, s16[24,2176]{1,0:T(8,128)(2,1)S(1)}, u32[]{:S(2)}, u32[]{:S(2)}) collective-permute-start(s16[24,2176]{1,0:T(8,128)(2,1)S(1)} %get-tuple-element.36.refs_6_.refs_1_), channel_id=1, source_target_pairs={{0,24},{8,16},{16,8},{24,0},{1,25},{9,17},{17,9},{25,1},{2,26},{10... | collective-permute-start | bytes 313352 | tf_op jit(solution)/shard_map/ppermute | solution.py:285
  4.9 0.7 %collective-permute-start = (s16[24,2176]{1,0:T(8,128)(2,1)S(1)}, s16[24,2176]{1,0:T(8,128)(2,1)S(1)}, u32[]{:S(2)}, u32[]{:S(2)}) collective-permute-start(s16[24,2176]{1,0:T(8,128)(2,1)S(1)} %get-tuple-element.36.refs_6_.refs_1_), channel_id=1, source_target_pairs={{0,8},{8,0},{16,24},{24,16},{1,9},{9,1},{17,25},{25,17},{2,10},{10... | collective-permute-start | bytes 313352 | tf_op jit(solution)/shard_map/ppermute | solution.py:285
  5.6 0.3 shard_map.95
  5.9 0.1 collective-permute-start.4
  6.0 0.0 collective-permute-start.3
  6.0 0.2 shard_map.96
  6.2 1.7 %collective-permute-start.10 = (s16[24,4224]{1,0:T(8,128)(2,1)S(1)}, s16[24,4224]{1,0:T(8,128)(2,1)S(1)}, u32[]{:S(2)}, u32[]{:S(2)}) collective-permute-start(s16[24,4224]{1,0:T(8,128)(2,1)S(1)} %get-tuple-element.40.refs_4_.refs_1_), channel_id=1, source_target_pairs={{0,24},{8,16},{16,8},{24,0},{1,25},{9,17},{17,9},{25,1},{2,26},{10... | collective-permute-start | bytes 608264 | tf_op jit(solution)/shard_map/ppermute | solution.py:285
  7.9 0.3 collective-permute-done.1.refs_3_
  8.2 0.2 collective-permute-start.9
  8.5 0.0 collective-permute-done.refs_2_
  8.5 0.2 shard_map.97
  8.7 2.5 %collective-permute-start.2 = (s16[24,2176]{1,0:T(8,128)(2,1)S(1)}, s16[24,2176]{1,0:T(8,128)(2,1)S(1)}, u32[]{:S(2)}, u32[]{:S(2)}) collective-permute-start(s16[24,2176]{1,0:T(8,128)(2,1)S(1)} %get-tuple-element.42.refs_4_.refs_1_), channel_id=1, source_target_pairs={{0,4},{4,0},{1,5},{5,1},{2,6},{6,2},{3,7},{7,3},{8,12},{12,8},{9,1... | collective-permute-start | bytes 313352 | tf_op jit(solution)/shard_map/ppermute | solution.py:285
  11.2 0.0 collective-permute-done.4.refs_3_
  11.2 0.0 collective-permute-done.3.refs_2_
  11.2 0.3 shard_map.98
  11.5 1.7 %collective-permute-start.5 = (s16[24,2176]{1,0:T(8,128)(2,1)S(1)}, s16[24,2176]{1,0:T(8,128)(2,1)S(1)}, u32[]{:S(2)}, u32[]{:S(2)}) collective-permute-start(s16[24,2176]{1,0:T(8,128)(2,1)S(1)} %get-tuple-element.44.refs_3_.own), channel_id=1, source_target_pairs={{0,4},{4,0},{1,5},{5,1},{2,6},{6,2},{3,7},{7,3},{8,12},{12,8},{9,1... | collective-permute-start | bytes 313352 | tf_op jit(solution)/shard_map/ppermute | solution.py:285
  13.2 0.2 shard_map.99
  13.4 0.4 %collective-permute-start.8 = (s16[24,4224]{1,0:T(8,128)(2,1)S(1)}, s16[24,4224]{1,0:T(8,128)(2,1)S(1)}, u32[]{:S(2)}, u32[]{:S(2)}) collective-permute-start(s16[24,4224]{1,0:T(8,128)(2,1)S(1)} %get-tuple-element.45.refs_3_.refs_1_), channel_id=1, source_target_pairs={{0,4},{4,0},{1,5},{5,1},{2,6},{6,2},{3,7},{7,3},{8,12},{12,8},{9,1... | collective-permute-start | bytes 608264 | tf_op jit(solution)/shard_map/ppermute | solution.py:285
  13.8 0.8 %collective-permute-done.2.refs_2_ = s16[24,2176]{1,0:T(8,128)(2,1)S(1)} collective-permute-done((s16[24,2176]{1,0:T(8,128)(2,1)S(1)}, s16[24,2176]{1,0:T(8,128)(2,1)S(1)}, u32[]{:S(2)}, u32[]{:S(2)}) %collective-permute-start.2) | collective-permute-done | bytes 104480 | tf_op jit(solution)/shard_map/ppermute | solution.py:285
  14.6 0.1 shard_map.100
  14.8 3.0 %collective-permute-start.7 = (bf16[24,2048]{1,0:T(8,128)(2,1)S(1)}, bf16[24,2048]{1,0:T(8,128)(2,1)S(1)}, u32[]{:S(2)}, u32[]{:S(2)}) collective-permute-start(bf16[24,2048]{1,0:T(8,128)(2,1)S(1)} %get-tuple-element.48.early_rounded), channel_id=1, source_target_pairs={{0,2},{1,3},{2,0},{3,1},{4,6},{5,7},{6,4},{7,5},{8,10},{9,11},{10,... | collective-permute-start | bytes 294920 | tf_op jit(solution)/shard_map/ppermute | solution.py:285
  17.8 0.1 shard_map.101
  17.9 1.6 %collective-permute-start.6 = (bf16[24,4096]{1,0:T(8,128)(2,1)S(1)}, bf16[24,4096]{1,0:T(8,128)(2,1)S(1)}, u32[]{:S(2)}, u32[]{:S(2)}) collective-permute-start(bf16[24,4096]{1,0:T(8,128)(2,1)S(1)} %get-tuple-element.50.refs_4_.refs_1_.refs_2_), channel_id=1, source_target_pairs={{0,1},{1,0},{2,3},{3,2},{4,5},{5,4},{6,7},{7,6},{8,9},{9,8},{10,11... | collective-permute-start | bytes 589832 | tf_op jit(solution)/shard_map/ppermute | solution.py:285
  19.6 2.2 %collective-permute-start.12 = (bf16[24,2048]{1,0:T(8,128)(2,1)S(1)}, bf16[24,2048]{1,0:T(8,128)(2,1)S(1)}, u32[]{:S(2)}, u32[]{:S(2)}) collective-permute-start(bf16[24,2048]{1,0:T(8,128)(2,1)S(1)} %shard_map.106), channel_id=1, source_target_pairs={{0,2},{1,3},{2,0},{3,1},{4,6},{5,7},{6,4},{7,5},{8,10},{9,11},{10,... | collective-permute-start | bytes 294920 | tf_op jit(solution)/shard_map/ppermute | solution.py:285
  21.8 0.0 collective-permute-done.9.refs_2_
  21.8 0.5 %shard_map.102 = (f32[24,4096]{1,0:T(8,128)S(1)}, s16[24,4224]{1,0:T(8,128)(2,1)S(1)}) custom-call(f32[24,4096]{1,0:T(8,128)S(1)} %get-tuple-element.52.refs_0_, s16[24,4224]{1,0:T(8,128)(2,1)S(1)} %get-tuple-element.40.refs_4_.refs_1_, s16[24,4224]{1,0:T(8,128)(2,1)S(1)} %collective-permute-done.9.refs_2_, ...), custom_call_target="tpu_custom_call" | custom-call | tf_op jit(solution)/shard_map/pallas_call | solution.py:272
  22.3 1.6 %collective-permute-start.13 = (s16[24,4224]{1,0:T(8,128)(2,1)S(1)}, s16[24,4224]{1,0:T(8,128)(2,1)S(1)}, u32[]{:S(2)}, u32[]{:S(2)}) collective-permute-start(s16[24,4224]{1,0:T(8,128)(2,1)S(1)} %get-tuple-element.53.refs_3_.refs_1_), channel_id=1, source_target_pairs={{0,4},{4,0},{1,5},{5,1},{2,6},{6,2},{3,7},{7,3},{8,12},{12,8},{9,1... | collective-permute-start | bytes 608264 | tf_op jit(solution)/shard_map/ppermute | solution.py:285
  23.8 0.0 collective-permute-done.8.refs_2_
  23.8 0.3 %shard_map.103 = (f32[24,4096]{1,0:T(8,128)S(1)}, s16[24,4224]{1,0:T(8,128)(2,1)S(1)}, s16[24,4224]{1,0:T(8,128)(2,1)S(1)}) custom-call(f32[24,4096]{1,0:T(8,128)S(1)} %get-tuple-element.51.refs_0_, s16[24,4224]{1,0:T(8,128)(2,1)S(1)} %get-tuple-element.45.refs_3_.refs_1_, s16[24,4224]{1,0:T(8,128)(2,1)S(1)} %collective-permute-done.8.refs_2_, ...), custom_call_target="tpu_custom_call" | custom-call | tf_op jit(solution)/shard_map/pallas_call | solution.py:272
  24.2 0.1 collective-permute-start.15
  24.3 0.0 collective-permute-done.7.refs_0_
  24.3 0.5 %collective-permute-start.11 = (bf16[24,2048]{1,0:T(8,128)(2,1)S(1)}, bf16[24,2048]{1,0:T(8,128)(2,1)S(1)}, u32[]{:S(2)}, u32[]{:S(2)}) collective-permute-start(bf16[24,2048]{1,0:T(8,128)(2,1)S(1)} %shard_map.105.refs_0_.refs_4_), channel_id=1, source_target_pairs={{0,1},{1,0},{2,3},{3,2},{4,5},{5,4},{6,7},{7,6},{8,9},{9,8},{10,11... | collective-permute-start | bytes 294920 | tf_op jit(solution)/shard_map/ppermute | solution.py:285
  24.8 1.2 %collective-permute-done.12.refs_0_ = bf16[24,2048]{1,0:T(8,128)(2,1)S(1)} collective-permute-done((bf16[24,2048]{1,0:T(8,128)(2,1)S(1)}, bf16[24,2048]{1,0:T(8,128)(2,1)S(1)}, u32[]{:S(2)}, u32[]{:S(2)}) %collective-permute-start.12) | collective-permute-done | bytes 98336 | tf_op jit(solution)/shard_map/ppermute | solution.py:285
  26.0 2.6 %collective-permute-start.16 = (bf16[24,2048]{1,0:T(8,128)(2,1)S(1)}, bf16[24,2048]{1,0:T(8,128)(2,1)S(1)}, u32[]{:S(2)}, u32[]{:S(2)}) collective-permute-start(bf16[24,2048]{1,0:T(8,128)(2,1)S(1)} %shard_map.108.refs_3_.refs_6_.refs_1_), channel_id=1, source_target_pairs={{0,1},{1,0},{2,3},{3,2},{4,5},{5,4},{6,7},{7,6},{8,9},{9,8},{10,11... | collective-permute-start | bytes 294920 | tf_op jit(solution)/shard_map/ppermute | solution.py:285
  28.6 0.0 collective-permute-done.13.refs_2_
  28.6 0.0 collective-permute-start.14
  28.6 0.9 %shard_map.109 = (f32[24,4096]{1,0:T(8,128)}, f32[8,128]{1,0:T(8,128)S(1)}) custom-call(f32[24,4096]{1,0:T(8,128)S(1)} %get-tuple-element.56.refs_0_, s16[24,4224]{1,0:T(8,128)(2,1)S(1)} %get-tuple-element.53.refs_3_.refs_1_, s16[24,4224]{1,0:T(8,128)(2,1)S(1)} %collective-permute-done.13.refs_2_, bf16[24,2048]{1,0:T(8,128)(2,1)S(1)} %shard_map.108.refs_3_.refs_6_.refs_1_), custom_call_target="tpu_custom_call" | custom-call | flops 4000000000 | tf_op jit(solution)/shard_map/pallas_call | solution.py:272
  29.5 0.0 collective-permute-done.11.refs_5_
  29.5 1.0 %shard_map.110 = (bf16[4,24,4096]{2,1,0:T(8,128)(2,1)}, f32[24,4096]{1,0:T(8,128)}, f32[8,128]{1,0:T(8,128)S(1)}) custom-call(f32[24,2048]{1,0:T(8,128)S(1)} %get-tuple-element.46.refs_0_, f32[24,2048]{1,0:T(8,128)S(1)} %get-tuple-element.49.refs_1_, bf16[24,4096]{1,0:T(8,128)(2,1)S(1)} %get-tuple-element.50.refs_4_.refs_1_.refs_2_, ...), custom_call_target="tpu_custom_call" | custom-call | flops 2000000000 | tf_op jit(solution)/shard_map/pallas_call | solution.py:272
  30.5 1.6 %collective-permute-done.16.refs_1_.refs_5_ = bf16[24,2048]{1,0:T(8,128)(2,1)S(1)} collective-permute-done((bf16[24,2048]{1,0:T(8,128)(2,1)S(1)}, bf16[24,2048]{1,0:T(8,128)(2,1)S(1)}, u32[]{:S(2)}, u32[]{:S(2)}) %collective-permute-start.16) | collective-permute-done | bytes 98336 | tf_op jit(solution)/shard_map/ppermute | solution.py:285
  32.1 1.0 %shard_map.113 = (bf16[4,24,4096]{2,1,0:T(8,128)(2,1)}, f32[24,4096]{1,0:T(8,128)}) custom-call(bf16[4,24,4096]{2,1,0:T(8,128)(2,1)} %get-tuple-element.60.refs_0_, f32[24,4096]{1,0:T(8,128)S(1)} %get-tuple-element.61.refs_1_, s16[24,4224]{1,0:T(8,128)(2,1)S(1)} %get-tuple-element.54.refs_0_.refs_2_, ...), custom_call_target="tpu_custom_call", output_to_operand_aliasing={{0}: (0, {})} | custom-call | tf_op jit(solution)/shard_map/pallas_call | solution.py:272
  (17 shorter events, 0.0 us)
Async XLA Ops:
  0.6 0.9 %copy-start.3 = (bf16[1,1,24,4096]{3,2,1,0:T(8,128)(2,1)S(1)}, bf16[1,1,24,4096]{3,2,1,0:T(8,128)(2,1)}, u32[]{:S(2)}) copy-start(bf16[1,1,24,4096]{3,2,1,0:T(8,128)(2,1)} %param.9) | copy-start | bytes 589828
  0.6 1.1 %copy-start.2 = (f32[1,1,24,4096]{3,2,1,0:T(8,128)S(1)}, f32[1,1,24,4096]{3,2,1,0:T(8,128)}, u32[]{:S(2)}) copy-start(f32[1,1,24,4096]{3,2,1,0:T(8,128)} %param.8) | copy-start | bytes 1179652
  0.7 1.2 %copy-start.1 = (f32[1,1,24,4096]{3,2,1,0:T(8,128)S(1)}, f32[1,1,24,4096]{3,2,1,0:T(8,128)}, u32[]{:S(2)}) copy-start(f32[1,1,24,4096]{3,2,1,0:T(8,128)} %param.7) | copy-start | bytes 1179652
  0.7 1.3 %copy-start = (f32[1,1,24,4096]{3,2,1,0:T(8,128)S(1)}, f32[1,1,24,4096]{3,2,1,0:T(8,128)}, u32[]{:S(2)}) copy-start(f32[1,1,24,4096]{3,2,1,0:T(8,128)} %param.6) | copy-start | bytes 1179652
  1.4 0.8 %copy-start.4 = (s32[1,1,8]{2,1,0:T(1,128)S(1)}, s32[1,1,8]{2,1,0:T(1,128)}, u32[]{:S(2)}) copy-start(s32[1,1,8]{2,1,0:T(1,128)} %param.10) | copy-start | bytes 100
  2.5 5.8 %collective-permute-start.1 = (s16[24,2176]{1,0:T(8,128)(2,1)S(1)}, s16[24,2176]{1,0:T(8,128)(2,1)S(1)}, u32[]{:S(2)}, u32[]{:S(2)}) collective-permute-start(s16[24,2176]{1,0:T(8,128)(2,1)S(1)} %get-tuple-element.36.refs_6_.refs_1_), channel_id=1, source_target_pairs={{0,24},{8,16},{16,8},{24,0},{1,25},{9,17},{17,9},{25,1},{2,26},{10... | collective-permute-start | bytes 313352 | tf_op jit(solution)/shard_map/ppermute | solution.py:285
  4.9 3.5 %collective-permute-start = (s16[24,2176]{1,0:T(8,128)(2,1)S(1)}, s16[24,2176]{1,0:T(8,128)(2,1)S(1)}, u32[]{:S(2)}, u32[]{:S(2)}) collective-permute-start(s16[24,2176]{1,0:T(8,128)(2,1)S(1)} %get-tuple-element.36.refs_6_.refs_1_), channel_id=1, source_target_pairs={{0,8},{8,0},{16,24},{24,16},{1,9},{9,1},{17,25},{25,17},{2,10},{10... | collective-permute-start | bytes 313352 | tf_op jit(solution)/shard_map/ppermute | solution.py:285
  5.9 5.3 %collective-permute-start.4 = (s16[24,2176]{1,0:T(8,128)(2,1)S(1)}, s16[24,2176]{1,0:T(8,128)(2,1)S(1)}, u32[]{:S(2)}, u32[]{:S(2)}) collective-permute-start(s16[24,2176]{1,0:T(8,128)(2,1)S(1)} %get-tuple-element.39.refs_3_.refs_1_), channel_id=1, source_target_pairs={{0,24},{8,16},{16,8},{24,0},{1,25},{9,17},{17,9},{25,1},{2,26},{10... | collective-permute-start | bytes 313352 | tf_op jit(solution)/shard_map/ppermute | solution.py:285
  6.0 5.2 %collective-permute-start.3 = (s16[24,2176]{1,0:T(8,128)(2,1)S(1)}, s16[24,2176]{1,0:T(8,128)(2,1)S(1)}, u32[]{:S(2)}, u32[]{:S(2)}) collective-permute-start(s16[24,2176]{1,0:T(8,128)(2,1)S(1)} %get-tuple-element.39.refs_3_.refs_1_), channel_id=1, source_target_pairs={{0,8},{8,0},{16,24},{24,16},{1,9},{9,1},{17,25},{25,17},{2,10},{10... | collective-permute-start | bytes 313352 | tf_op jit(solution)/shard_map/ppermute | solution.py:285
  6.2 13.3 %collective-permute-start.10 = (s16[24,4224]{1,0:T(8,128)(2,1)S(1)}, s16[24,4224]{1,0:T(8,128)(2,1)S(1)}, u32[]{:S(2)}, u32[]{:S(2)}) collective-permute-start(s16[24,4224]{1,0:T(8,128)(2,1)S(1)} %get-tuple-element.40.refs_4_.refs_1_), channel_id=1, source_target_pairs={{0,24},{8,16},{16,8},{24,0},{1,25},{9,17},{17,9},{25,1},{2,26},{10... | collective-permute-start | bytes 608264 | tf_op jit(solution)/shard_map/ppermute | solution.py:285
  8.2 13.6 %collective-permute-start.9 = (s16[24,4224]{1,0:T(8,128)(2,1)S(1)}, s16[24,4224]{1,0:T(8,128)(2,1)S(1)}, u32[]{:S(2)}, u32[]{:S(2)}) collective-permute-start(s16[24,4224]{1,0:T(8,128)(2,1)S(1)} %get-tuple-element.40.refs_4_.refs_1_), channel_id=1, source_target_pairs={{0,8},{8,0},{16,24},{24,16},{1,9},{9,1},{17,25},{25,17},{2,10},{10... | collective-permute-start | bytes 608264 | tf_op jit(solution)/shard_map/ppermute | solution.py:285
  8.7 5.9 %collective-permute-start.2 = (s16[24,2176]{1,0:T(8,128)(2,1)S(1)}, s16[24,2176]{1,0:T(8,128)(2,1)S(1)}, u32[]{:S(2)}, u32[]{:S(2)}) collective-permute-start(s16[24,2176]{1,0:T(8,128)(2,1)S(1)} %get-tuple-element.42.refs_4_.refs_1_), channel_id=1, source_target_pairs={{0,4},{4,0},{1,5},{5,1},{2,6},{6,2},{3,7},{7,3},{8,12},{12,8},{9,1... | collective-permute-start | bytes 313352 | tf_op jit(solution)/shard_map/ppermute | solution.py:285
  11.5 6.3 %collective-permute-start.5 = (s16[24,2176]{1,0:T(8,128)(2,1)S(1)}, s16[24,2176]{1,0:T(8,128)(2,1)S(1)}, u32[]{:S(2)}, u32[]{:S(2)}) collective-permute-start(s16[24,2176]{1,0:T(8,128)(2,1)S(1)} %get-tuple-element.44.refs_3_.own), channel_id=1, source_target_pairs={{0,4},{4,0},{1,5},{5,1},{2,6},{6,2},{3,7},{7,3},{8,12},{12,8},{9,1... | collective-permute-start | bytes 313352 | tf_op jit(solution)/shard_map/ppermute | solution.py:285
  13.4 10.4 %collective-permute-start.8 = (s16[24,4224]{1,0:T(8,128)(2,1)S(1)}, s16[24,4224]{1,0:T(8,128)(2,1)S(1)}, u32[]{:S(2)}, u32[]{:S(2)}) collective-permute-start(s16[24,4224]{1,0:T(8,128)(2,1)S(1)} %get-tuple-element.45.refs_3_.refs_1_), channel_id=1, source_target_pairs={{0,4},{4,0},{1,5},{5,1},{2,6},{6,2},{3,7},{7,3},{8,12},{12,8},{9,1... | collective-permute-start | bytes 608264 | tf_op jit(solution)/shard_map/ppermute | solution.py:285
  14.8 9.5 %collective-permute-start.7 = (bf16[24,2048]{1,0:T(8,128)(2,1)S(1)}, bf16[24,2048]{1,0:T(8,128)(2,1)S(1)}, u32[]{:S(2)}, u32[]{:S(2)}) collective-permute-start(bf16[24,2048]{1,0:T(8,128)(2,1)S(1)} %get-tuple-element.48.early_rounded), channel_id=1, source_target_pairs={{0,2},{1,3},{2,0},{3,1},{4,6},{5,7},{6,4},{7,5},{8,10},{9,11},{10,... | collective-permute-start | bytes 294920 | tf_op jit(solution)/shard_map/ppermute | solution.py:285
  17.9 11.6 %collective-permute-start.6 = (bf16[24,4096]{1,0:T(8,128)(2,1)S(1)}, bf16[24,4096]{1,0:T(8,128)(2,1)S(1)}, u32[]{:S(2)}, u32[]{:S(2)}) collective-permute-start(bf16[24,4096]{1,0:T(8,128)(2,1)S(1)} %get-tuple-element.50.refs_4_.refs_1_.refs_2_), channel_id=1, source_target_pairs={{0,1},{1,0},{2,3},{3,2},{4,5},{5,4},{6,7},{7,6},{8,9},{9,8},{10,11... | collective-permute-start | bytes 589832 | tf_op jit(solution)/shard_map/ppermute | solution.py:285
  19.6 6.4 %collective-permute-start.12 = (bf16[24,2048]{1,0:T(8,128)(2,1)S(1)}, bf16[24,2048]{1,0:T(8,128)(2,1)S(1)}, u32[]{:S(2)}, u32[]{:S(2)}) collective-permute-start(bf16[24,2048]{1,0:T(8,128)(2,1)S(1)} %shard_map.106), channel_id=1, source_target_pairs={{0,2},{1,3},{2,0},{3,1},{4,6},{5,7},{6,4},{7,5},{8,10},{9,11},{10,... | collective-permute-start | bytes 294920 | tf_op jit(solution)/shard_map/ppermute | solution.py:285
  22.3 6.3 %collective-permute-start.13 = (s16[24,4224]{1,0:T(8,128)(2,1)S(1)}, s16[24,4224]{1,0:T(8,128)(2,1)S(1)}, u32[]{:S(2)}, u32[]{:S(2)}) collective-permute-start(s16[24,4224]{1,0:T(8,128)(2,1)S(1)} %get-tuple-element.53.refs_3_.refs_1_), channel_id=1, source_target_pairs={{0,4},{4,0},{1,5},{5,1},{2,6},{6,2},{3,7},{7,3},{8,12},{12,8},{9,1... | collective-permute-start | bytes 608264 | tf_op jit(solution)/shard_map/ppermute | solution.py:285
  24.2 8.0 %collective-permute-start.15 = (s16[24,4224]{1,0:T(8,128)(2,1)S(1)}, s16[24,4224]{1,0:T(8,128)(2,1)S(1)}, u32[]{:S(2)}, u32[]{:S(2)}) collective-permute-start(s16[24,4224]{1,0:T(8,128)(2,1)S(1)} %get-tuple-element.54.refs_0_.refs_2_), channel_id=1, source_target_pairs={{0,24},{8,16},{16,8},{24,0},{1,25},{9,17},{17,9},{25,1},{2,26},{10... | collective-permute-start | bytes 608264 | tf_op jit(solution)/shard_map/ppermute | solution.py:285
  24.3 5.2 %collective-permute-start.11 = (bf16[24,2048]{1,0:T(8,128)(2,1)S(1)}, bf16[24,2048]{1,0:T(8,128)(2,1)S(1)}, u32[]{:S(2)}, u32[]{:S(2)}) collective-permute-start(bf16[24,2048]{1,0:T(8,128)(2,1)S(1)} %shard_map.105.refs_0_.refs_4_), channel_id=1, source_target_pairs={{0,1},{1,0},{2,3},{3,2},{4,5},{5,4},{6,7},{7,6},{8,9},{9,8},{10,11... | collective-permute-start | bytes 294920 | tf_op jit(solution)/shard_map/ppermute | solution.py:285
  26.0 6.1 %collective-permute-start.16 = (bf16[24,2048]{1,0:T(8,128)(2,1)S(1)}, bf16[24,2048]{1,0:T(8,128)(2,1)S(1)}, u32[]{:S(2)}, u32[]{:S(2)}) collective-permute-start(bf16[24,2048]{1,0:T(8,128)(2,1)S(1)} %shard_map.108.refs_3_.refs_6_.refs_1_), channel_id=1, source_target_pairs={{0,1},{1,0},{2,3},{3,2},{4,5},{5,4},{6,7},{7,6},{8,9},{9,8},{10,11... | collective-permute-start | bytes 294920 | tf_op jit(solution)/shard_map/ppermute | solution.py:285
  28.6 3.5 %collective-permute-start.14 = (s16[24,4224]{1,0:T(8,128)(2,1)S(1)}, s16[24,4224]{1,0:T(8,128)(2,1)S(1)}, u32[]{:S(2)}, u32[]{:S(2)}) collective-permute-start(s16[24,4224]{1,0:T(8,128)(2,1)S(1)} %shard_map.111), channel_id=1, source_target_pairs={{0,8},{8,0},{16,24},{24,16},{1,9},{9,1},{17,25},{25,17},{2,10},{10... | collective-permute-start | bytes 608264 | tf_op jit(solution)/shard_map/ppermute | solution.py:285
